TPU v7x, 512 devices: a whole 4x4x16 slice. The times are simulated.
512 devices in a mesh: dp: 4 (over y), seq: 128 (over x, z, core).
Axes of the slice: x: 4, y: 4, z: 16, core: 2. Of those that a mesh axis runs over, the one named last changes fastest.
Arguments:
- queries: bfloat16 [4, 16384, 1792], P('dp', 'seq'), may hold values from -132 to 132, as said below
- keys: bfloat16 [4, 16384, 256], P('dp', 'seq'), may hold values from -6 to 6, as said below
- values: bfloat16 [4, 16384, 256], P('dp', 'seq'), may hold values from -6 to 6
- grad_out: bfloat16 [4, 16384, 1792], P('dp', 'seq'), may hold values from -24 to 24
- beacon_keys: bfloat16 [4, 1024, 256], P('dp', 'seq'), may hold values from -6 to 6
- beacon_values: bfloat16 [4, 1024, 256], P('dp', 'seq'), may hold values from -6 to 6
- beacon_hidden: bfloat16 [4, 1024, 3584], P('dp', 'seq'), may hold values from -6 to 6
- order: int32 [128], replicated, may hold values from 0 to 127, each once
- ratio: int32 [128], replicated, may hold values from 16 to 32, as said below
Outputs:
- query_grads: bfloat16 [4, 16384, 1792], P('dp', 'seq')
- key_grads: bfloat16 [4, 16384, 256], P('dp', 'seq')
- value_grads: bfloat16 [4, 16384, 256], P('dp', 'seq')
- beacon_key_grads: bfloat16 [4, 1024, 256], P('dp', 'seq')
- beacon_value_grads: bfloat16 [4, 1024, 256], P('dp', 'seq')
- key_weight_grad: float32 [3584, 256], P(('dp', 'seq'))
Inputs may be any that keep to these rules, and one draw needn't show every extreme that they name: queries lie in this range. keys lie in this range. `ratio`: each entry is 16 or 32, and both occur. `order`: a permutation of 0 to 127.
All inputs are finite; a program needn't handle non-finite values.
Results may differ from a plain program's by a relative error of at most 0.012.
Values may be sent and summed in bfloat16 or wider, within the bound.
No kernel may reach another device: no remote copies, remote signals or barrier semaphores. Data moves between devices by JAX's collectives and lax.ppermute only.
A program may use at most 64 MiB of HBM per device.

v0:
```python
import math

import jax
import jax.numpy as jnp
from jax import lax
from jax.sharding import PartitionSpec as P

QH = 14
KVH = 2
HD = 128


NEG = -1e30


def per_device(
    queries, keys, values, grad_out, beacon_keys, beacon_values, beacon_hidden, order, ratio
):
    nseq = lax.axis_size("seq")
    me = lax.axis_index("seq")
    span_len = queries.shape[1]
    slots = beacon_keys.shape[1]
    total = nseq * slots
    groups = QH // KVH
    scale = 1.0 / math.sqrt(HD)
    query = queries[0].reshape(span_len, KVH, groups, HD)
    upstream = grad_out[0].reshape(span_len, KVH, groups, HD)
    local_keys = keys[0].reshape(span_len, KVH, HD)
    local_values = values[0].reshape(span_len, KVH, HD)
    peers = jnp.arange(nseq, dtype=jnp.int32)
    mine = jnp.sum(jnp.where(peers == me, order, 0))
    positions = jnp.arange(span_len, dtype=jnp.int32)
    causal = positions[:, None] >= positions[None, :]

    def visible(start, count):
        beacon_rows = start + jnp.arange(count, dtype=jnp.int32)
        owner = beacon_rows // slots
        span = jnp.sum(jnp.where(owner[:, None] == peers[None, :], order[None, :], 0), axis=1)
        rate = jnp.sum(jnp.where(span[:, None] == peers[None, :], ratio[None, :], 0), axis=1)
        return ((span < mine) & (beacon_rows % slots < span_len // rate))[None, :]

    def logits(part_keys, mask):
        scores = (
            jnp.einsum("ikgd,jkd->kgij", query, part_keys, preferred_element_type=jnp.float32)
            * scale
        )
        return jnp.where(mask, scores, NEG)

    def stats_step(carry, part_keys, mask):
        top, mass = carry
        scores = logits(part_keys, mask)
        newtop = jnp.maximum(top, jnp.max(scores, axis=-1))
        mass = mass * jnp.exp(top - newtop) + jnp.sum(jnp.exp(scores - newtop[..., None]), axis=-1)
        return (newtop, mass)

    def split_piece(pieces):
        count = pieces[0].shape[0]
        return (pieces[0].reshape(count, KVH, HD), pieces[1].reshape(count, KVH, HD), count)

    def beacon_stats(carry, pieces, start):
        part_keys, part_values, count = split_piece(pieces)
        return stats_step(carry, part_keys, visible(start, count))

    start_stats = (
        jnp.full((KVH, groups, span_len), NEG, jnp.float32),
        jnp.zeros((KVH, groups, span_len), jnp.float32),
    )
    start_stats = stats_step(start_stats, local_keys, causal)
    gathered = (
        lax.all_gather(beacon_keys[0], "seq", axis=0, tiled=True),
        lax.all_gather(beacon_values[0], "seq", axis=0, tiled=True),
    )
    block = min(512, total)

    def sweep(step_fn, init):

        def advance(index, carry):
            first = index * block
            pieces = (
                lax.dynamic_slice_in_dim(gathered[0], first, block, 0),
                lax.dynamic_slice_in_dim(gathered[1], first, block, 0),
            )
            return step_fn(carry, pieces, first)

        return lax.fori_loop(0, total // block, advance, init)

    top, mass = sweep(beacon_stats, start_stats)
    lse = top + jnp.log(mass)

    def probs_of(part_keys, mask):
        return jnp.where(mask, jnp.exp(logits(part_keys, mask) - lse[..., None]), 0.0)

    def delta_step(acc, part_keys, part_values, mask):
        probs = probs_of(part_keys, mask)
        dprobs = jnp.einsum(
            "ikgd,jkd->kgij", upstream, part_values, preferred_element_type=jnp.float32
        )
        return acc + jnp.sum(probs * dprobs, axis=-1)

    def beacon_deltas(acc, pieces, start):
        part_keys, part_values, count = split_piece(pieces)
        return delta_step(acc, part_keys, part_values, visible(start, count))

    start_delta = delta_step(
        jnp.zeros((KVH, groups, span_len), jnp.float32), local_keys, local_values, causal
    )
    delta = sweep(beacon_deltas, start_delta)

    def grad_step(acc_q, part_keys, part_values, mask):
        probs = probs_of(part_keys, mask)
        dprobs = jnp.einsum(
            "ikgd,jkd->kgij", upstream, part_values, preferred_element_type=jnp.float32
        )
        dscores = (probs * (dprobs - delta[..., None])).astype(jnp.bfloat16)
        probs_b = probs.astype(jnp.bfloat16)
        acc_q = acc_q + jnp.einsum(
            "kgij,jkd->ikgd", dscores, part_keys, preferred_element_type=jnp.float32
        )
        grad_k = (
            jnp.einsum("kgij,ikgd->jkd", dscores, query, preferred_element_type=jnp.float32) * scale
        )
        grad_v = jnp.einsum("kgij,ikgd->jkd", probs_b, upstream, preferred_element_type=jnp.float32)
        return (acc_q, grad_k, grad_v)

    def beacon_grads(carry, pieces, start):
        acc_q, dense_k, dense_v = carry
        part_keys, part_values, count = split_piece(pieces)
        acc_q, grad_k, grad_v = grad_step(acc_q, part_keys, part_values, visible(start, count))
        dense_k = lax.dynamic_update_slice_in_dim(dense_k, grad_k, start, 0)
        dense_v = lax.dynamic_update_slice_in_dim(dense_v, grad_v, start, 0)
        return (acc_q, dense_k, dense_v)

    acc_q, own_k, own_v = grad_step(
        jnp.zeros((span_len, KVH, groups, HD), jnp.float32), local_keys, local_values, causal
    )
    start_grads = (
        acc_q,
        jnp.zeros((total, KVH, HD), jnp.float32),
        jnp.zeros((total, KVH, HD), jnp.float32),
    )
    acc_q, dense_k, dense_v = sweep(beacon_grads, start_grads)
    query_grads = (acc_q * scale).reshape(span_len, QH * HD).astype(jnp.bfloat16)
    key_grads = own_k.reshape(span_len, KVH * HD).astype(jnp.bfloat16)
    value_grads = own_v.reshape(span_len, KVH * HD).astype(jnp.bfloat16)
    summed_k = jnp.sum(
        lax.all_to_all(
            dense_k.reshape(nseq, slots, KVH * HD), "seq", split_axis=0, concat_axis=0, tiled=True
        ),
        axis=0,
    )
    summed_v = jnp.sum(
        lax.all_to_all(
            dense_v.reshape(nseq, slots, KVH * HD), "seq", split_axis=0, concat_axis=0, tiled=True
        ),
        axis=0,
    )
    beacon_key_grads = summed_k.astype(jnp.bfloat16)
    beacon_value_grads = summed_v.astype(jnp.bfloat16)
    hidden_rows = beacon_hidden[0]
    key_weight_grad = lax.psum_scatter(
        lax.dot_general(
            hidden_rows,
            beacon_key_grads,
            (((0,), (0,)), ((), ())),
            preferred_element_type=jnp.float32,
        ),
        ("dp", "seq"),
        scatter_dimension=0,
        tiled=True,
    )
    return (
        query_grads[None],
        key_grads[None],
        value_grads[None],
        beacon_key_grads[None],
        beacon_value_grads[None],
        key_weight_grad,
    )


def solution(mesh):
    placed = (
        P("dp", "seq", None),
        P("dp", "seq", None),
        P("dp", "seq", None),
        P("dp", "seq", None),
        P("dp", "seq", None),
        P("dp", "seq", None),
        P("dp", "seq", None),
        P(),
        P(),
    )
    return jax.shard_map(
        per_device,
        mesh=mesh,
        in_specs=placed,
        out_specs=(
            P("dp", "seq", None),
            P("dp", "seq", None),
            P("dp", "seq", None),
            P("dp", "seq", None),
            P("dp", "seq", None),
            P(("dp", "seq"), None),
        ),
        check_vma=False,
    )
```

profile of v0, /device:TPU:1, one launch (start us, length us, event | category | flops | bytes accessed | tf_op | source)
XLA Modules:
  0.0 817.6 jit_solution(4958812039691848840)
XLA Ops:
  7.2 0.9 reshape_squeeze.12
  8.1 0.9 reshape_squeeze.14
  9.0 1.3 copy.99
  10.5 1.3 copy.104
  11.8 1.0 copy.110
  12.8 91.0 %all-gather = bf16[1,1024,256]{2,1,0:T(8,128)(2,1)S(1)} all-gather(bf16[1,8,256]{2,1,0:T(8,128)(2,1)S(1)} %copy-done.21), channel_id=2, replica_groups=mesh['dp'=4,'seq'=128] {'seq'}, dimensions={1}, use_global_device_ids=true | all-gather | bytes 528384 | tf_op jit(solution)/shard_map/all_gather | solution.py:70
  104.0 81.9 %all-gather.1 = bf16[1,1024,256]{2,1,0:T(8,128)(2,1)S(1)} all-gather(bf16[1,8,256]{2,1,0:T(8,128)(2,1)S(1)} %copy-done.22), channel_id=3, replica_groups=mesh['dp'=4,'seq'=128] {'seq'}, dimensions={1}, use_global_device_ids=true | all-gather | bytes 528384 | tf_op jit(solution)/shard_map/all_gather | solution.py:71
  187.3 6.3 while.60
  188.6 1.0 bitcast_reduce_fusion.2
  189.6 0.8 fusion.112
  191.8 1.0 bitcast_reduce_fusion.2
  192.8 0.8 fusion.112
  193.7 1.2 multiply_reduce_fusion
  194.9 10.0 %while.61 = (s32[]{:T(128)}, f32[2,7,128]{2,1,0:T(8,128)S(1)}, s32[128]{0:T(128)}, s32[]{:T(128)}, s32[128]{0:T(128)}, /*index=5*/bf16[1024,256]{0,1:T(8,128)(2,...) while((s32[]{:T(128)}, f32[2,7,128]{2,1,0:T(8,128)S(1)}, ...), condition=%wide.region_14.15_spmd.clone.clone, body=%wide.region_10.14_spmd.clone.clone.sunk | while | flops 475679232 | bytes 11746555 | solution.py:85
  194.9 1.0 select_reduce_fusion.14
  195.9 0.9 select_reduce_fusion.15
  198.3 1.5 fusion.118
  199.9 0.9 select_reduce_fusion.14
  200.9 0.9 select_reduce_fusion.15
  203.3 1.5 fusion.118
  204.9 1.0 multiply_convert_fusion.1
  206.7 1.3 convolution_bitcast_fusion.3
  207.9 1.5 copy.113
  209.4 1.3 broadcast.383.clone2
  210.7 1.3 broadcast.383.clone
  212.0 17.6 %while.62 = (s32[]{:T(128)}, f32[128,2,7,128]{0,3,2,1:T(8,128)S(1)}, f32[1024,2,128]{2,1,0:T(2,128)}, f32[1024,2,128]{2,1,0:T(2,128)}, bf16[1024,256]{0,1:T(8,12...) while((s32[]{:T(128)}, ...), condition=%wide.region_18.19_spmd.clone.clone, body=%wide.region_15.18_spmd.clone.clone.sunk | while | flops 1186187776 | bytes 43816816 | solution.py:85
  214.1 1.0 fusion.132
  215.1 1.9 fusion.130
  218.6 0.9 copy_dynamic-update-slice_fusion.3
  219.5 1.0 copy-done.5
  222.9 1.0 fusion.132
  223.9 1.9 fusion.130
  227.3 0.9 copy_dynamic-update-slice_fusion.3
  228.2 1.0 copy-done.5
  229.6 3.0 reshape.203
  232.6 9.7 %all-to-all-start = ((f32[128,8,256]{2,1,0:T(8,128)}), f32[128,8,256]{2,1,0:T(8,128)S(1)}, u32[]{:S(2)}, u32[]{:S(2)}) async-start(f32[128,8,256]{2,1,0:T(8,128)} %reshape.203), calls=%async_computation | async-start | bytes 2097152 | tf_op jit(solution)/shard_map/all_to_all | solution.py:146
  242.4 3.0 reshape.204
  245.4 51.3 %all-to-all-done = f32[128,8,256]{2,1,0:T(8,128)S(1)} async-done(((f32[128,8,256]{2,1,0:T(8,128)}), f32[128,8,256]{2,1,0:T(8,128)S(1)}, u32[]{:S(2)}, u32[]{:S(2)}) %all-to-all-start) | async-done | bytes 1048608 | tf_op jit(solution)/shard_map/all_to_all | solution.py:146
  296.7 1.0 copy-done.3
  297.7 8.5 %all-to-all-start.1 = ((f32[128,8,256]{2,1,0:T(8,128)}), f32[128,8,256]{2,1,0:T(8,128)S(1)}, u32[]{:S(2)}, u32[]{:S(2)}) async-start(f32[128,8,256]{2,1,0:T(8,128)} %reshape.204), calls=%async_computation.1 | async-start | bytes 2097152 | tf_op jit(solution)/shard_map/all_to_all | solution.py:152
  306.3 1.4 reduce_sum.184
  307.7 2.5 convolution_bitcast_fusion.2
  310.2 1.3 fusion.48
  312.3 1.3 fusion.47
  314.5 1.0 copy.122
  315.5 47.2 %all-to-all-done.1 = f32[128,8,256]{2,1,0:T(8,128)S(1)} async-done(((f32[128,8,256]{2,1,0:T(8,128)}), f32[128,8,256]{2,1,0:T(8,128)S(1)}, u32[]{:S(2)}, u32[]{:S(2)}) %all-to-all-start.1) | async-done | bytes 1048608 | tf_op jit(solution)/shard_map/all_to_all | solution.py:152
  363.4 445.6 %all-reduce.3.cloned.1.call-done = f32[3584,256]{0,1:T(8,128)} async-done(((f32[3584,256]{0,1:T(8,128)}), f32[3584,256]{0,1:T(8,128)}) %all-reduce.3.cloned.1.call-update) | async-done | bytes 3670032
  809.1 1.0 constant_dynamic-slice_fusion.5
  (118 shorter events, 19.1 us)
Async XLA Ops:
  7.2 300.5 %copy-start = (bf16[1,8,3584]{2,1,0:T(8,128)(2,1)S(1)}, bf16[1,8,3584]{2,1,0:T(8,128)(2,1)}, u32[]{:S(2)}) copy-start(bf16[1,8,3584]{2,1,0:T(8,128)(2,1)} %param.21) | copy-start | bytes 172036
  7.2 5.6 copy-start.21
  7.2 96.8 %copy-start.22 = (bf16[1,8,256]{2,1,0:T(8,128)(2,1)S(1)}, bf16[1,8,256]{2,1,0:T(8,128)(2,1)}, u32[]{:S(2)}) copy-start(bf16[1,8,256]{2,1,0:T(8,128)(2,1)} %param.20) | copy-start | bytes 12292
  10.2 176.2 %copy-start.1 = (bf16[1,128,1792]{1,2,0:T(8,128)(2,1)}, bf16[1,128,1792]{1,2,0:T(8,128)(2,1)S(1)}, u32[]{:S(2)}) copy-start(bf16[1,128,1792]{1,2,0:T(8,128)(2,1)S(1)} %copy.99) | copy-start | bytes 1376260
  10.5 176.1 %copy-start.13 = (s32[128]{0:T(128)S(1)}, s32[128]{0:T(128)}, u32[]{:S(2)}) copy-start(s32[128]{0:T(128)} %param.22) | copy-start | bytes 1540
  10.5 176.8 %copy-start.15 = (s32[128]{0:T(128)S(1)}, s32[128]{0:T(128)}, u32[]{:S(2)}) copy-start(s32[128]{0:T(128)} %param.23) | copy-start | bytes 1540
  11.8 181.8 %copy-start.8 = (bf16[1,128,1792]{1,2,0:T(8,128)(2,1)}, bf16[1,128,1792]{1,2,0:T(8,128)(2,1)S(1)}, u32[]{:S(2)}) copy-start(bf16[1,128,1792]{1,2,0:T(8,128)(2,1)S(1)} %copy.104) | copy-start | bytes 1376260
  193.6 1.3 copy-start.17
  194.9 10.0 %copy-start.10 = (f32[2,7,128,128]{2,3,1,0:T(8,128)S(1)}, f32[2,7,128,128]{2,3,1,0:T(8,128)}, u32[]{:S(2)}) copy-start(f32[2,7,128,128]{2,3,1,0:T(8,128)} %get-tuple-element.1309) | copy-start | bytes 2752516
  194.9 3.4 copy-start.18
  194.9 3.4 copy-start.11
  199.9 3.4 copy-start.18
  199.9 3.4 copy-start.11
  204.9 7.1 copy-start.14
  204.9 7.1 copy-start.16
  204.9 7.1 copy-start.19
  205.9 0.8 copy-start.9
  212.0 2.0 copy-start.12
  217.0 1.2 copy-start.4
  217.0 1.5 copy-start.6
  219.4 1.0 copy-start.5
  219.5 1.4 copy-start.7
  220.8 2.0 copy-start.12
  225.8 1.2 copy-start.4
  225.8 1.5 copy-start.6
  228.2 1.0 copy-start.5
  228.2 1.4 copy-start.7
  232.6 64.1 %all-to-all-start = ((f32[128,8,256]{2,1,0:T(8,128)}), f32[128,8,256]{2,1,0:T(8,128)S(1)}, u32[]{:S(2)}, u32[]{:S(2)}) async-start(f32[128,8,256]{2,1,0:T(8,128)} %reshape.203), calls=%async_computation | async-start | bytes 2097152 | tf_op jit(solution)/shard_map/all_to_all | solution.py:146
  296.7 1.0 copy-start.3
  297.7 65.0 %all-to-all-start.1 = ((f32[128,8,256]{2,1,0:T(8,128)}), f32[128,8,256]{2,1,0:T(8,128)S(1)}, u32[]{:S(2)}, u32[]{:S(2)}) async-start(f32[128,8,256]{2,1,0:T(8,128)} %reshape.204), calls=%async_computation.1 | async-start | bytes 2097152 | tf_op jit(solution)/shard_map/all_to_all | solution.py:152
  306.2 502.9 %all-reduce.3.cloned.1.call-start = ((), (), s32[]{:S(2)}) async-start(), calls=%async_computation.2 | async-start | bytes 7340032
  307.6 2.6 copy-start.20
  307.6 4.7 copy-start.2
Sparse Core Ops, SparseCore 0:
  312.5 496.5 all-reduce.2
where the time goes:
time: 819 us; the launch traced here: 818 us
  waiting for transfers between devices  544 us (66%)
  blocking collectives  173 us (21%)
  local copies, waits for them, and re-layouts  27.5 us (3%)
  matrix products  24 us (3%)
  starting transfers between devices  18.3 us (2%)
  other arithmetic  16 us (2%)
  between operations  14.3 us (2%)
    unnamed x2, waiting for transfers between devices  446 us
    all_gather x1, blocking collectives, per_device(): lax.all_gather(beacon_keys[0], 'seq', axis=0, tiled=True)  91 us
    all_gather x1, blocking collectives, per_device(): lax.all_gather(beacon_values[0], 'seq', axis=0, tiled=True)  81.9 us
    all_to_all x1, waiting for transfers between devices, per_device(): lax.all_to_all(dense_k.reshape(nseq, slots, KVH * HD), 'seq', split_axis=...  51.3 us
    all_to_all x1, waiting for transfers between devices, per_device(): lax.all_to_all(dense_v.reshape(nseq, slots, KVH * HD), 'seq', split_axis=...  47.2 us
  transfers between devices with their start and end apart: 3, of which 3 were waited for; matrix products, arithmetic and copies ran while one was open for 2% of the time, Pallas kernels for 0%

commit v1 on v0

v1 whole, which is shorter than its diff:
```python
import functools
import math

import jax
import jax.numpy as jnp
from jax import lax
from jax.experimental import pallas as pl
from jax.experimental.pallas import tpu as pltpu
from jax.sharding import Mesh
from jax.sharding import PartitionSpec as P

QH = 14
KVH = 2
HD = 128
GROUPS = QH // KVH
NEG = -1e30
SCALE = 1.0 / math.sqrt(HD)
LOG2E = math.log2(math.e)
CORES = 2
F32 = jnp.float32
BF16 = jnp.bfloat16


def grid_of(mesh):
    devices = mesh.devices
    dp, seq = devices.shape
    nx = 4 if seq == 128 else 2
    return dp, nx, seq // (nx * CORES)


def visible_bias(order_row, ratio_row, mine, core, nx, nz, slots, span):
    nseq = order_row.shape[1]
    t = lax.broadcasted_iota(jnp.int32, (nseq, nseq), 0)
    picks = jnp.where(order_row == t, 1.0, 0.0).astype(F32)
    rates = jnp.broadcast_to(ratio_row.astype(F32), (8, nseq))
    rate = jnp.dot(rates, picks, preferred_element_type=F32)[:1]
    cost = jnp.where(order_row < mine, rate, 4.0 * span)
    count = nx * nz * slots
    row = lax.broadcasted_iota(jnp.int32, (count, nseq), 0)
    lane = lax.broadcasted_iota(jnp.int32, (count, nseq), 1)
    owner = (row // slots) * CORES + core
    own_cost = jnp.sum(jnp.where(owner == lane, cost, 0.0), axis=1, keepdims=True)
    slot = lax.broadcasted_iota(jnp.int32, (count, 1), 0) % slots
    return jnp.where((slot + 1).astype(F32) * own_cost <= float(span), 0.0, NEG)


def attention_kernel(
    nx, nz, slots, span,
    place, order_s, order_row, ratio_row, q, up, k, v, near_k, near_v, far_k, far_v,
    dq, dk, dv, keep, send,
    bias, kcat, vcat, qcat, ucat, probs, dscores,
):
    half = nx * nz * slots
    per_x = nz * slots
    core = place[2]
    me = (place[0] * nz + place[1]) * CORES + core

    @pl.when(pl.program_id(0) == 0)
    def _():
        mine = order_s[me]
        args = (order_row[...], ratio_row[...], mine)
        near = visible_bias(*args, core, nx, nz, slots, span)
        far = visible_bias(*args, 1 - core, nx, nz, slots, span)
        bias[0:half, :] = jnp.broadcast_to(near, (half, HD))
        bias[half : 2 * half, :] = jnp.broadcast_to(far, (half, HD))

    kcat[0:span, :] = k[...]
    vcat[0:span, :] = v[...]
    for i in range(nx):
        lo = span + i * per_x
        kcat[lo : lo + per_x, :] = near_k[i, 0:per_x, :]
        vcat[lo : lo + per_x, :] = near_v[i, 0:per_x, :]
        lo += half
        kcat[lo : lo + per_x, :] = far_k[i, 0:per_x, :]
        vcat[lo : lo + per_x, :] = far_v[i, 0:per_x, :]
    for h in range(GROUPS):
        qcat[h * span : (h + 1) * span, :] = q[:, h * HD : (h + 1) * HD]
        ucat[h * span : (h + 1) * span, :] = up[:, h * HD : (h + 1) * HD]

    key_row = lax.broadcasted_iota(jnp.int32, (span, span), 0)
    query_col = lax.broadcasted_iota(jnp.int32, (span, span), 1)
    causal = key_row <= query_col
    contract_last = (((1,), (1,)), ((), ()))
    for h in range(GROUPS):
        rows = slice(h * span, (h + 1) * span)
        s = lax.dot_general(kcat[...], qcat[rows, :], contract_last, preferred_element_type=F32)
        dp = lax.dot_general(vcat[...], ucat[rows, :], contract_last, preferred_element_type=F32)
        s = s * (SCALE * LOG2E)
        s = jnp.concatenate(
            [jnp.where(causal, s[0:span, :], NEG), s[span:, :] + bias[...]], axis=0
        )
        top = jnp.max(s, axis=0, keepdims=True)
        e = jnp.exp2(s - top)
        inv = 1.0 / jnp.sum(e, axis=0, keepdims=True)
        delta = jnp.sum(e * dp, axis=0, keepdims=True) * inv
        p = e * inv
        probs[:, rows] = p.astype(BF16)
        dscores[:, rows] = (p * (dp - delta)).astype(BF16)

    full_k = (
        lax.dot_general(
            dscores[...], qcat[...], (((1,), (0,)), ((), ())), preferred_element_type=F32
        )
        * SCALE
    )
    full_v = lax.dot_general(
        probs[...], ucat[...], (((1,), (0,)), ((), ())), preferred_element_type=F32
    )
    dk[...] = full_k[0:span, :].astype(BF16)
    dv[...] = full_v[0:span, :].astype(BF16)
    keep[0] = full_k[span : span + half, :]
    keep[1] = full_v[span : span + half, :]
    send[0] = full_k[span + half :, :].astype(BF16)
    send[1] = full_v[span + half :, :].astype(BF16)
    dqt = (
        lax.dot_general(
            kcat[...], dscores[...], (((0,), (0,)), ((), ())), preferred_element_type=F32
        )
        * SCALE
    )
    for h in range(GROUPS):
        dq[:, h * HD : (h + 1) * HD] = dqt[:, h * span : (h + 1) * span].T.astype(BF16)


def attention(place, order, ratio, q, up, k, v, near, far, nx, nz, slots):
    span = q.shape[0]
    half = nx * nz * slots
    nseq = order.shape[0]
    rows = near.shape[1]
    keys = span + 2 * half
    smem = pl.BlockSpec(memory_space=pltpu.SMEM)
    row_spec = pl.BlockSpec((1, nseq), lambda g: (0, 0))
    wide = pl.BlockSpec((span, GROUPS * HD), lambda g: (0, g))
    slim = pl.BlockSpec((span, HD), lambda g: (0, g))
    beacon_k = pl.BlockSpec((nx, rows, HD), lambda g: (0, 0, g))
    beacon_v = pl.BlockSpec((nx, rows, HD), lambda g: (0, 0, KVH + g))
    part = pl.BlockSpec((2, half, HD), lambda g: (0, 0, g))
    flops = 5 * 2 * QH * span * keys * HD
    return pl.pallas_call(
        functools.partial(attention_kernel, nx, nz, slots, span),
        grid=(KVH,),
        in_specs=[
            smem, smem, row_spec, row_spec, wide, wide, slim, slim,
            beacon_k, beacon_v, beacon_k, beacon_v,
        ],
        out_specs=[wide, slim, slim, part, part],
        out_shape=[
            jax.ShapeDtypeStruct((span, QH * HD), BF16),
            jax.ShapeDtypeStruct((span, KVH * HD), BF16),
            jax.ShapeDtypeStruct((span, KVH * HD), BF16),
            jax.ShapeDtypeStruct((2, half, KVH * HD), F32),
            jax.ShapeDtypeStruct((2, half, KVH * HD), BF16),
        ],
        scratch_shapes=[
            pltpu.VMEM((2 * half, HD), F32),
            pltpu.VMEM((keys, HD), BF16),
            pltpu.VMEM((keys, HD), BF16),
            pltpu.VMEM((GROUPS * span, HD), BF16),
            pltpu.VMEM((GROUPS * span, HD), BF16),
            pltpu.VMEM((keys, GROUPS * span), BF16),
            pltpu.VMEM((keys, GROUPS * span), BF16),
        ],
        compiler_params=pltpu.CompilerParams(vmem_limit_bytes=48 * 1024 * 1024),
        cost_estimate=pl.CostEstimate(
            flops=flops, bytes_accessed=4 * 1024 * 1024, transcendentals=QH * span * keys
        ),
        name="attention",
    )(
        place, order, order.reshape(1, nseq), ratio.reshape(1, nseq),
        q, up, k, v, near, near, far, far,
    )


def spread_kernel(nx, per_x, keep, got, out):
    total_k = (keep[0] + got[0].astype(F32)).astype(BF16)
    total_v = (keep[1] + got[1].astype(F32)).astype(BF16)
    half = nx * per_x
    for i in range(nx):
        out[i, 0:half, :] = total_k
        out[i, half : half + per_x, :] = total_v[i * per_x : (i + 1) * per_x, :]


def spread(keep, got, nx):
    _, half, width = keep.shape
    per_x = half // nx
    return pl.pallas_call(
        functools.partial(spread_kernel, nx, per_x),
        out_shape=jax.ShapeDtypeStruct((nx, half + per_x, width), BF16),
        compiler_params=pltpu.CompilerParams(vmem_limit_bytes=32 * 1024 * 1024),
        cost_estimate=pl.CostEstimate(flops=0, bytes_accessed=4 * 1024 * 1024, transcendentals=0),
        name="spread",
    )(keep, got)


def weight_kernel(nx, nz, slots, ndp, rows_out, place, got, hidden, terms, weights, total):
    per_x = nz * slots
    half = nx * per_x
    width = got.shape[2]
    key_sum = got[0, 0:half, :].astype(F32)
    value_sum = got[0, half : half + per_x, :].astype(F32)
    for i in range(1, nx):
        key_sum = key_sum + got[i, 0:half, :].astype(F32)
        value_sum = value_sum + got[i, half : half + per_x, :].astype(F32)
    total[...] = key_sum
    mine = total[pl.ds(pl.multiple_of(place[0] * per_x, per_x), per_x), :]
    terms[:, 0:width] = mine.astype(BF16)
    terms[:, width:] = value_sum.astype(BF16)
    ordered = jnp.concatenate(
        [
            total[x * per_x + z * slots : x * per_x + (z + 1) * slots, :]
            for z in range(nz)
            for x in range(nx)
        ],
        axis=0,
    ).astype(BF16)
    parts = hidden.shape[1]
    lanes = hidden.shape[3]
    products = [
        lax.dot_general(
            hidden[:, part].reshape(half, lanes),
            ordered,
            (((0,), (0,)), ((), ())),
            preferred_element_type=F32,
        )
        for part in range(parts)
    ]
    product = jnp.concatenate(products, axis=0).astype(BF16)
    count = ndp * CORES * nz * 8
    row = lax.broadcasted_iota(jnp.int32, (count, parts * lanes), 0)
    column = lax.broadcasted_iota(jnp.int32, (count, parts * lanes), 1)
    item = row % 8
    z = (row // 8) % nz
    core = (row // (8 * nz)) % CORES
    y = row // (8 * nz * CORES)
    source = ((y * nz + z) * CORES + core) * rows_out + item
    picks = jnp.where((source == column) & (item < rows_out), 1.0, 0.0).astype(BF16)
    weights[...] = jnp.dot(picks, product, preferred_element_type=F32).astype(BF16)


def weight_terms(place, got, hidden, nx, nz, slots, ndp, rows_out):
    per_x = nz * slots
    width = got.shape[2]
    count = ndp * CORES * nz * 8
    vmem = pl.BlockSpec(memory_space=pltpu.VMEM)
    return pl.pallas_call(
        functools.partial(weight_kernel, nx, nz, slots, ndp, rows_out),
        in_specs=[pl.BlockSpec(memory_space=pltpu.SMEM), vmem, vmem],
        out_specs=[vmem, vmem],
        out_shape=[
            jax.ShapeDtypeStruct((per_x, 2 * width), BF16),
            jax.ShapeDtypeStruct((count, width), BF16),
        ],
        scratch_shapes=[pltpu.VMEM((nx * per_x, width), F32)],
        compiler_params=pltpu.CompilerParams(vmem_limit_bytes=48 * 1024 * 1024),
        cost_estimate=pl.CostEstimate(
            flops=2 * count * nx * per_x * width * 3,
            bytes_accessed=4 * 1024 * 1024,
            transcendentals=0,
        ),
        name="weight_terms",
    )(place, got, hidden)


def join_kernel(terms, weights, out):
    width = weights.shape[2]
    total = weights[0].astype(F32)
    for i in range(1, weights.shape[0]):
        total = total + weights[i].astype(F32)
    out[:, 0 : 2 * width] = terms[...]
    out[:, 2 * width :] = total.astype(BF16)


def join(terms, weights):
    rows, width = terms.shape
    return pl.pallas_call(
        join_kernel,
        out_shape=jax.ShapeDtypeStruct((rows, width + weights.shape[2]), BF16),
        cost_estimate=pl.CostEstimate(flops=0, bytes_accessed=1024 * 1024, transcendentals=0),
        name="join",
    )(terms, weights)


def per_device(
    nx, nz,
    queries, keys, values, grad_out, beacon_keys, beacon_values, beacon_hidden, order, ratio,
):
    ndp = lax.axis_size("dp")
    span = queries.shape[1]
    slots, width = beacon_keys.shape[1:]
    model = beacon_hidden.shape[2]
    rows_out = model // (ndp * nx * nz * CORES)
    place = jnp.stack([lax.axis_index("x"), lax.axis_index("z"), lax.axis_index("core")])
    place = place.astype(jnp.int32)

    mine = jnp.concatenate([beacon_keys[0], beacon_values[0]], axis=1)
    over_z = lax.all_to_all(
        jnp.broadcast_to(mine[None], (nz, slots, 2 * width)), "z", 0, 0, tiled=True
    )
    columns = model // nx
    padded = -(-columns // (2 * width)) * (2 * width)
    parts = padded // (2 * width)
    hidden = beacon_hidden[0].reshape(slots, ndp, nx, model // (ndp * nx))
    hidden = hidden.transpose(2, 0, 1, 3).reshape(nx, slots, columns)
    hidden = jnp.pad(hidden, ((0, 0), (0, 0), (0, padded - columns)))
    hidden = hidden.reshape(nx, slots, parts, 2 * width).transpose(0, 2, 1, 3)
    hidden = hidden.reshape(nx, parts * slots, 2 * width)
    message = jnp.concatenate(
        [jnp.broadcast_to(over_z.reshape(1, nz * slots, 2 * width), (nx, nz * slots, 2 * width)), hidden],
        axis=1,
    )
    near = lax.all_to_all(message, "x", 0, 0, tiled=True)
    far = lax.ppermute(near, "core", [(0, 1), (1, 0)])
    hidden = near[:, nz * slots :].reshape(nx, parts, slots, 2 * width)
    hidden = hidden.transpose(1, 0, 2, 3).reshape(1, parts, nx * slots, 2 * width)
    hidden = lax.all_gather(hidden, "z", axis=0, tiled=True)

    dq, dk, dv, keep, send = attention(
        place, order, ratio, queries[0], grad_out[0], keys[0], values[0], near, far, nx, nz, slots
    )

    got = lax.ppermute(send, "core", [(0, 1), (1, 0)])
    got = lax.all_to_all(spread(keep, got, nx), "x", 0, 0, tiled=True)
    terms, weights = weight_terms(place, got, hidden, nx, nz, slots, ndp, rows_out)
    weights = weights.reshape(ndp * CORES, nz * 8, width)
    weights = lax.all_to_all(weights, ("dp", "core"), 0, 0, tiled=True)
    last = join(terms, weights).reshape(nz, 8, 3 * width)
    last = lax.all_to_all(last, "z", 0, 0, tiled=True)
    sums = jnp.sum(last.astype(F32), axis=0)
    beacon_dk = sums[:slots, :width].astype(BF16)
    beacon_dv = sums[:slots, width : 2 * width].astype(BF16)
    weight_grad = sums[:rows_out, 2 * width :]
    return (dq[None], dk[None], dv[None], beacon_dk[None], beacon_dv[None], weight_grad)


def solution(mesh):
    ndp, nx, nz = grid_of(mesh)
    fine = Mesh(mesh.devices.reshape(ndp, nx, nz, CORES), ("dp", "x", "z", "core"))
    seq = ("x", "z", "core")
    split = P("dp", seq, None)
    return jax.shard_map(
        functools.partial(per_device, nx, nz),
        mesh=fine,
        in_specs=(split,) * 7 + (P(), P()),
        out_specs=(split,) * 5 + (P(("dp",) + seq, None),),
        check_vma=False,
    )
```

time: 819 us -> 170 us (0.21)
  the two profiles are of different devices: /device:TPU:1 before, /device:TPU:2 now
where the time goes in v1:
time: 170 us; the launch traced here: 169 us
  waiting for transfers between devices  58.4 us (34%)
  blocking collectives  50.2 us (30%)
  starting transfers between devices  24.1 us (14%)
  Pallas kernels  16.4 us (10%)
  between operations  14.2 us (8%)
  local copies, waits for them, and re-layouts  4.89 us (3%)
    all_gather x1, waiting for transfers between devices, per_device(): hidden = lax.all_gather(hidden, 'z', axis=0, tiled=True)  41.8 us
    all_to_all x1, blocking collectives, per_device(): last = lax.all_to_all(last, 'z', 0, 0, tiled=True)  23.9 us
    all_to_all x1, starting transfers between devices, per_device(): lax.all_to_all(jnp.broadcast_to(mine[None], (nz, slots, 2 * width)), 'z',...  15.2 us
    all_to_all x1, blocking collectives, per_device(): weights = lax.all_to_all(weights, ('dp', 'core'), 0, 0, tiled=True)  14.6 us
    all_to_all x1, waiting for transfers between devices, per_device(): lax.all_to_all(jnp.broadcast_to(mine[None], (nz, slots, 2 * width)), 'z',...  13.5 us
    all_to_all x1, blocking collectives, per_device(): near = lax.all_to_all(message, 'x', 0, 0, tiled=True)  11.7 us
    pallas_call x1, Pallas kernels, attention(): pl.pallas_call(functools.partial(attention_kernel, nx, nz, slots, span),...  11.5 us
    all_to_all x1, starting transfers between devices, per_device(): got = lax.all_to_all(spread(keep, got, nx), 'x', 0, 0, tiled=True)  4.98 us
  transfers between devices with their start and end apart: 5, of which 4 were waited for; matrix products, arithmetic and copies ran while one was open for 1% of the time, Pallas kernels for 7%

profile of v1, /device:TPU:2, one launch (start us, length us, event | category | flops | bytes accessed | tf_op | source)
XLA Modules:
  0.0 169.1 jit_solution(17027035561058488405)
XLA Ops:
  7.2 0.7 pad_maximum_fusion.1
  7.9 0.7 broadcast_in_dim.28
  8.5 15.2 %all-to-all-start = ((bf16[16,8,512]{2,1,0:T(8,128)(2,1)}), bf16[16,8,512]{2,1,0:T(8,128)(2,1)S(1)}, u32[]{:S(2)}, u32[]{:S(2)}) async-start(bf16[16,8,512]{2,1,0:T(8,128)(2,1)} %broadcast_in_dim.28), calls=%async_computation | async-start | bytes 262144 | tf_op jit(solution)/shard_map/all_to_all | solution.py:296
  23.7 0.0 all-gather.2.cloned.1.call-start
  23.8 1.0 reshape_squeeze.3
  24.8 0.1 reshape.44
  24.9 13.5 %all-to-all-done = bf16[16,8,512]{2,1,0:T(8,128)(2,1)S(1)} async-done(((bf16[16,8,512]{2,1,0:T(8,128)(2,1)}), bf16[16,8,512]{2,1,0:T(8,128)(2,1)S(1)}, u32[]{:S(2)}, u32[]{:S(2)}) %all-to-all-start) | async-done | bytes 131104 | tf_op jit(solution)/shard_map/all_to_all | solution.py:296
  38.5 0.0 copy-start.2
  38.5 0.0 copy-start.3
  38.5 0.0 copy-start.4
  38.5 0.0 copy-start.5
  38.5 0.0 copy-start.6
  38.5 0.0 copy-start.7
  38.6 11.7 %all_to_all.25.near_k.near_v = bf16[4,144,512]{2,1,0:T(8,128)(2,1)S(1)} all-to-all(bf16[4,144,512]{2,1,0:T(8,128)(2,1)S(1)} %pad_maximum_fusion), channel_id=1, replica_groups=mesh['dp'=4,'x'=4,'z'=16,'core'=2] {'x'}, dimensions={0} | all-to-all | bytes 1179648 | tf_op jit(solution)/shard_map/all_to_all | solution.py:311
  50.3 1.9 %collective-permute-start = (bf16[4,144,512]{2,1,0:T(8,128)(2,1)S(1)}, bf16[4,144,512]{2,1,0:T(8,128)(2,1)S(1)}, u32[]{:S(2)}, u32[]{:S(2)}) collective-permute-start(bf16[4,144,512]{2,1,0:T(8,128)(2,1)S(1)} %all_to_all.25.near_k.near_v), channel_id=1, source_target_pairs={{0,1},{1,0},{2,3},{3,2},{4,5},{5,4},{6,7},{7,6},{8,9},{9,8},{10,11... | collective-permute-start | bytes 1769480 | tf_op jit(solution)/shard_map/ppermute | solution.py:312
  52.3 0.6 copy_bitcast_fusion
  52.9 0.0 all-gather.2.cloned.1.call-update
  52.9 0.1 pad_add_fusion.place
  53.0 1.2 collective-permute-done.far_k.far_v
  54.2 0.0 copy-done.2
  54.2 0.0 copy-done.3
  54.2 0.0 copy-done.4
  54.2 0.0 copy-done.5
  54.2 0.0 copy-done.6
  54.3 0.0 copy-done.7
  54.3 11.5 %attention.1 = (bf16[128,1792]{1,0:T(8,128)(2,1)}, bf16[128,256]{1,0:T(8,128)(2,1)}, bf16[128,256]{1,0:T(8,128)(2,1)}, f32[2,512,256]{2,1,0:T(8,128)S(1)}, bf16[2,512,256]{2,1,0:T(8,128)(2,1)S(1)}) custom-call(s32[3]{0:T(128)S(1)} %pad_add_fusion.place, s32[128]{0:T(128)S(1)} %copy-done.6, s32[1,128]{1,0:T(1,128)S(1)} %bitcast.41, s32[1,128]{1,0:T(1,128)S(1)} %bitcast.42, ...), custom_call_target="tpu_custom_call" | custom-call | flops 2642411520 | bytes 4194304 | tf_op jit(solution)/shard_map/attention/pallas_call | solution.py:139
  65.7 2.0 %collective-permute-start.1 = (bf16[2,512,256]{2,1,0:T(8,128)(2,1)S(1)}, bf16[2,512,256]{2,1,0:T(8,128)(2,1)S(1)}, u32[]{:S(2)}, u32[]{:S(2)}) collective-permute-start(bf16[2,512,256]{2,1,0:T(8,128)(2,1)S(1)} %get-tuple-element.17), channel_id=1, source_target_pairs={{0,1},{1,0},{2,3},{3,2},{4,5},{5,4},{6,7},{7,6},{8,9},{9,8},{10,11... | collective-permute-start | bytes 1572872 | tf_op jit(solution)/shard_map/ppermute | solution.py:321
  67.8 1.8 %collective-permute-done.1.got = bf16[2,512,256]{2,1,0:T(8,128)(2,1)S(1)} collective-permute-done((bf16[2,512,256]{2,1,0:T(8,128)(2,1)S(1)}, bf16[2,512,256]{2,1,0:T(8,128)(2,1)S(1)}, u32[]{:S(2)}, u32[]{:S(2)}) %collective-permute-start.1) | collective-permute-done | bytes 524320 | tf_op jit(solution)/shard_map/ppermute | solution.py:321
  69.5 1.2 spread.1
  70.7 5.0 %all-to-all-start.2 = ((bf16[4,640,256]{2,1,0:T(8,128)(2,1)}), bf16[4,640,256]{2,1,0:T(8,128)(2,1)S(1)}, u32[]{:S(2)}, u32[]{:S(2)}) async-start(bf16[4,640,256]{2,1,0:T(8,128)(2,1)} %spread.1), calls=%async_computation.2 | async-start | bytes 2621440 | tf_op jit(solution)/shard_map/all_to_all | solution.py:322
  75.7 41.8 %all-gather.2.cloned.1.call-done.hidden = bf16[16,2,32,512]{3,2,1,0:T(8,128)(2,1)} async-done(((bf16[1,2,32,512]{3,2,1,0:T(8,128)(2,1)}), bf16[16,2,32,512]{3,2,1,0:T(8,128)(2,1)}) %all-gather.2.cloned.1.call-update) | async-done | bytes 1048592 | tf_op jit(solution)/shard_map/all_gather | solution.py:315
  117.5 0.0 all-to-all-done.2.got
  117.5 0.0 copy-start.1
  117.5 1.2 copy-done.1
  118.8 1.8 %weight_terms.1 = (bf16[128,512]{1,0:T(8,128)(2,1)S(1)}, bf16[1024,256]{1,0:T(8,128)(2,1)S(1)}) custom-call(s32[3]{0:T(128)S(1)} %pad_add_fusion.place, bf16[4,640,256]{2,1,0:T(8,128)(2,1)S(1)} %all-to-all-done.2.got, bf16[16,2,32,512]{3,2,1,0:T(8,128)(2,1)S(1)} %copy-done.1), custom_call_target="tpu_custom_call" | custom-call | flops 805306368 | bytes 4194304 | tf_op jit(solution)/shard_map/weight_terms/pallas_call | solution.py:245
  120.6 0.0 copy-start
  120.6 14.6 %all_to_all.26.weights = bf16[8,128,256]{2,1,0:T(8,128)(2,1)} all-to-all(bf16[8,128,256]{2,1,0:T(8,128)(2,1)S(1)} %bitcast.36), channel_id=1, replica_groups=mesh['dp'=4,'x'=4,'z'=16,'core'=2] {'dp','core'}, dimensions={0} | all-to-all | bytes 1048576 | tf_op jit(solution)/shard_map/all_to_all | solution.py:325
  135.2 0.0 copy-done
  135.2 1.9 %join.1 = bf16[128,768]{1,0:T(8,128)(2,1)} custom-call(bf16[128,512]{1,0:T(8,128)(2,1)} %copy-done, bf16[8,128,256]{2,1,0:T(8,128)(2,1)} %all_to_all.26.weights), custom_call_target="tpu_custom_call" | custom-call | bytes 1048576 | tf_op jit(solution)/shard_map/join/pallas_call | solution.py:275
  137.1 23.9 %all_to_all.27 = bf16[16,8,768]{2,1,0:T(8,128)(2,1)S(1)} all-to-all(bf16[16,8,768]{2,1,0:T(8,128)(2,1)} %bitcast.43), channel_id=1, replica_groups=mesh['dp'=4,'x'=4,'z'=16,'core'=2] {'z'}, dimensions={0} | all-to-all | bytes 393216 | tf_op jit(solution)/shard_map/all_to_all | solution.py:327
  161.1 0.6 slice.21
  161.7 0.6 slice_bitcast_fusion.1
  (6 shorter events, 0.2 us)
Async XLA Ops:
  8.5 29.9 %all-to-all-start = ((bf16[16,8,512]{2,1,0:T(8,128)(2,1)}), bf16[16,8,512]{2,1,0:T(8,128)(2,1)S(1)}, u32[]{:S(2)}, u32[]{:S(2)}) async-start(bf16[16,8,512]{2,1,0:T(8,128)(2,1)} %broadcast_in_dim.28), calls=%async_computation | async-start | bytes 262144 | tf_op jit(solution)/shard_map/all_to_all | solution.py:296
  23.7 93.8 %all-gather.2.cloned.1.call-start = ((), (), s32[]{:S(2)}) async-start(), calls=%async_computation.5 | async-start | bytes 1114112 | tf_op jit(solution)/shard_map/all_gather | solution.py:315
  38.5 15.7 %copy-start.2 = (bf16[1,128,1792]{2,1,0:T(8,128)(2,1)S(1)}, bf16[1,128,1792]{2,1,0:T(8,128)(2,1)}, u32[]{:S(2)}) copy-start(bf16[1,128,1792]{2,1,0:T(8,128)(2,1)} %param.9) | copy-start | bytes 1376260
  38.5 15.7 %copy-start.3 = (bf16[1,128,1792]{2,1,0:T(8,128)(2,1)S(1)}, bf16[1,128,1792]{2,1,0:T(8,128)(2,1)}, u32[]{:S(2)}) copy-start(bf16[1,128,1792]{2,1,0:T(8,128)(2,1)} %param.12) | copy-start | bytes 1376260
  38.5 15.7 %copy-start.4 = (bf16[1,128,256]{2,1,0:T(8,128)(2,1)S(1)}, bf16[1,128,256]{2,1,0:T(8,128)(2,1)}, u32[]{:S(2)}) copy-start(bf16[1,128,256]{2,1,0:T(8,128)(2,1)} %param.10) | copy-start | bytes 196612
  38.5 15.7 %copy-start.5 = (bf16[1,128,256]{2,1,0:T(8,128)(2,1)S(1)}, bf16[1,128,256]{2,1,0:T(8,128)(2,1)}, u32[]{:S(2)}) copy-start(bf16[1,128,256]{2,1,0:T(8,128)(2,1)} %param.11) | copy-start | bytes 196612
  38.5 15.7 %copy-start.6 = (s32[128]{0:T(128)S(1)}, s32[128]{0:T(128)}, u32[]{:S(2)}) copy-start(s32[128]{0:T(128)} %order_s.1) | copy-start | bytes 1540
  38.5 15.7 %copy-start.7 = (s32[128]{0:T(128)S(1)}, s32[128]{0:T(128)}, u32[]{:S(2)}) copy-start(s32[128]{0:T(128)} %param.17) | copy-start | bytes 1540
  50.3 3.9 %collective-permute-start = (bf16[4,144,512]{2,1,0:T(8,128)(2,1)S(1)}, bf16[4,144,512]{2,1,0:T(8,128)(2,1)S(1)}, u32[]{:S(2)}, u32[]{:S(2)}) collective-permute-start(bf16[4,144,512]{2,1,0:T(8,128)(2,1)S(1)} %all_to_all.25.near_k.near_v), channel_id=1, source_target_pairs={{0,1},{1,0},{2,3},{3,2},{4,5},{5,4},{6,7},{7,6},{8,9},{9,8},{10,11... | collective-permute-start | bytes 1769480 | tf_op jit(solution)/shard_map/ppermute | solution.py:312
  65.7 3.8 %collective-permute-start.1 = (bf16[2,512,256]{2,1,0:T(8,128)(2,1)S(1)}, bf16[2,512,256]{2,1,0:T(8,128)(2,1)S(1)}, u32[]{:S(2)}, u32[]{:S(2)}) collective-permute-start(bf16[2,512,256]{2,1,0:T(8,128)(2,1)S(1)} %get-tuple-element.17), channel_id=1, source_target_pairs={{0,1},{1,0},{2,3},{3,2},{4,5},{5,4},{6,7},{7,6},{8,9},{9,8},{10,11... | collective-permute-start | bytes 1572872 | tf_op jit(solution)/shard_map/ppermute | solution.py:321
  70.7 46.8 %all-to-all-start.2 = ((bf16[4,640,256]{2,1,0:T(8,128)(2,1)}), bf16[4,640,256]{2,1,0:T(8,128)(2,1)S(1)}, u32[]{:S(2)}, u32[]{:S(2)}) async-start(bf16[4,640,256]{2,1,0:T(8,128)(2,1)} %spread.1), calls=%async_computation.2 | async-start | bytes 2621440 | tf_op jit(solution)/shard_map/all_to_all | solution.py:322
  117.5 1.2 copy-start.1
  120.6 14.6 %copy-start = (bf16[128,512]{1,0:T(8,128)(2,1)}, bf16[128,512]{1,0:T(8,128)(2,1)S(1)}, u32[]{:S(2)}) copy-start(bf16[128,512]{1,0:T(8,128)(2,1)S(1)} %get-tuple-element.18.terms) | copy-start | bytes 393220
Sparse Core Ops, SparseCore 0:
  53.0 64.4 all-gather.1

commit v2 on v1

v2 whole, which is shorter than its diff:
```python
import functools
import math

import jax
import jax.numpy as jnp
from jax import lax
from jax.experimental import pallas as pl
from jax.experimental.pallas import tpu as pltpu
from jax.sharding import Mesh
from jax.sharding import PartitionSpec as P

QH = 14
KVH = 2
HD = 128
GROUPS = QH // KVH
NEG = -1e30
SCALE = 1.0 / math.sqrt(HD)
LOG2E = math.log2(math.e)
CORES = 2
SUB = 8
F32 = jnp.float32
BF16 = jnp.bfloat16


def grid_of(mesh):
    dp, seq = mesh.devices.shape
    nx, nzl = (4, 4) if seq == 128 else (2, 2)
    return dp, nx, seq // (nx * nzl * CORES), nzl


def visible_bias(order_row, ratio_row, mine, core, nx, nz, slots, span):
    nseq = order_row.shape[1]
    t = lax.broadcasted_iota(jnp.int32, (nseq, nseq), 0)
    picks = jnp.where(order_row == t, 1.0, 0.0).astype(F32)
    rates = jnp.broadcast_to(ratio_row.astype(F32), (8, nseq))
    rate = jnp.dot(rates, picks, preferred_element_type=F32)[:1]
    cost = jnp.where(order_row < mine, rate, 4.0 * span)
    count = nx * nz * slots
    row = lax.broadcasted_iota(jnp.int32, (count, nseq), 0)
    lane = lax.broadcasted_iota(jnp.int32, (count, nseq), 1)
    owner = (row // slots) * CORES + core
    own_cost = jnp.sum(jnp.where(owner == lane, cost, 0.0), axis=1, keepdims=True)
    slot = lax.broadcasted_iota(jnp.int32, (count, 1), 0) % slots
    return jnp.where((slot + 1).astype(F32) * own_cost <= float(span), 0.0, NEG)


def attention_kernel(
    nx, nzh, nzl, slots, span,
    place, order_s, order_row, ratio_row, q, up, k, v, near_k, near_v, far_k, far_v,
    dq, dk, dv, keep, send,
    bias, kcat, vcat, qcat, ucat, probs, dscores,
):
    nz = nzh * nzl
    half = nx * nz * slots
    core = place[2]
    me = (place[0] * nz + place[1]) * CORES + core

    @pl.when(pl.program_id(0) == 0)
    def _():
        mine = order_s[me]
        args = (order_row[...], ratio_row[...], mine)
        near = visible_bias(*args, core, nx, nz, slots, span)
        far = visible_bias(*args, 1 - core, nx, nz, slots, span)
        bias[0:half, :] = jnp.broadcast_to(near, (half, HD))
        bias[half : 2 * half, :] = jnp.broadcast_to(far, (half, HD))

    for cat, own, near, far in ((kcat, k, near_k, far_k), (vcat, v, near_v, far_v)):
        cat[0:span, :] = own[...]
        cat[span : span + half, :] = near[...]
        cat[span + half :, :] = far[...]
    for h in range(GROUPS):
        qcat[h * span : (h + 1) * span, :] = q[:, h * HD : (h + 1) * HD]
        ucat[h * span : (h + 1) * span, :] = up[:, h * HD : (h + 1) * HD]

    key_row = lax.broadcasted_iota(jnp.int32, (span, span), 0)
    query_col = lax.broadcasted_iota(jnp.int32, (span, span), 1)
    causal = key_row <= query_col
    contract_last = (((1,), (1,)), ((), ()))
    for h in range(GROUPS):
        rows = slice(h * span, (h + 1) * span)
        s = lax.dot_general(kcat[...], qcat[rows, :], contract_last, preferred_element_type=F32)
        dp = lax.dot_general(vcat[...], ucat[rows, :], contract_last, preferred_element_type=F32)
        s = s * (SCALE * LOG2E)
        s = jnp.concatenate(
            [jnp.where(causal, s[0:span, :], NEG), s[span:, :] + bias[...]], axis=0
        )
        top = jnp.max(s, axis=0, keepdims=True)
        e = jnp.exp2(s - top)
        inv = 1.0 / jnp.sum(e, axis=0, keepdims=True)
        delta = jnp.sum(e * dp, axis=0, keepdims=True) * inv
        p = e * inv
        probs[:, rows] = p.astype(BF16)
        dscores[:, rows] = (p * (dp - delta)).astype(BF16)

    full_k = (
        lax.dot_general(
            dscores[...], qcat[...], (((1,), (0,)), ((), ())), preferred_element_type=F32
        )
        * SCALE
    )
    full_v = lax.dot_general(
        probs[...], ucat[...], (((1,), (0,)), ((), ())), preferred_element_type=F32
    )
    dk[...] = full_k[0:span, :].astype(BF16)
    dv[...] = full_v[0:span, :].astype(BF16)
    for kind, full in ((0, full_k), (1, full_v)):
        for out, lo in ((keep, span), (send, span + half)):
            rows = full[lo : lo + half, :].reshape(nx, nzh, nzl, slots, HD)
            out[kind] = jnp.swapaxes(rows, 1, 2).reshape(half, HD).astype(out.dtype)
    dqt = (
        lax.dot_general(
            kcat[...], dscores[...], (((0,), (0,)), ((), ())), preferred_element_type=F32
        )
        * SCALE
    )
    for h in range(GROUPS):
        dq[:, h * HD : (h + 1) * HD] = dqt[:, h * span : (h + 1) * span].T.astype(BF16)


def attention(place, order, ratio, q, up, k, v, near, far, nx, nzh, nzl, slots):
    span = q.shape[0]
    half = nx * nzh * nzl * slots
    nseq = order.shape[0]
    keys = span + 2 * half
    row_spec = pl.BlockSpec((1, nseq), lambda g: (0, 0))
    wide = pl.BlockSpec((span, GROUPS * HD), lambda g: (0, g))
    slim = pl.BlockSpec((span, HD), lambda g: (0, g))
    beacon_k = pl.BlockSpec((half, HD), lambda g: (0, g))
    beacon_v = pl.BlockSpec((half, HD), lambda g: (0, KVH + g))
    part = pl.BlockSpec((2, half, HD), lambda g: (0, 0, g))
    flops = 5 * 2 * QH * span * keys * HD
    return pl.pallas_call(
        functools.partial(attention_kernel, nx, nzh, nzl, slots, span),
        grid=(KVH,),
        in_specs=[
            SMEM, SMEM, row_spec, row_spec, wide, wide, slim, slim,
            beacon_k, beacon_v, beacon_k, beacon_v,
        ],
        out_specs=[wide, slim, slim, part, part],
        out_shape=[
            jax.ShapeDtypeStruct((span, QH * HD), BF16),
            jax.ShapeDtypeStruct((span, KVH * HD), BF16),
            jax.ShapeDtypeStruct((span, KVH * HD), BF16),
            jax.ShapeDtypeStruct((2, half, KVH * HD), F32),
            jax.ShapeDtypeStruct((2, half, KVH * HD), BF16),
        ],
        scratch_shapes=[
            pltpu.VMEM((2 * half, HD), F32),
            pltpu.VMEM((keys, HD), BF16),
            pltpu.VMEM((keys, HD), BF16),
            pltpu.VMEM((GROUPS * span, HD), BF16),
            pltpu.VMEM((GROUPS * span, HD), BF16),
            pltpu.VMEM((keys, GROUPS * span), BF16),
            pltpu.VMEM((keys, GROUPS * span), BF16),
        ],
        compiler_params=pltpu.CompilerParams(vmem_limit_bytes=48 * 1024 * 1024),
        cost_estimate=pl.CostEstimate(
            flops=flops, bytes_accessed=4 * 1024 * 1024, transcendentals=QH * span * keys
        ),
        name="attention",
    )(
        place, order, order.reshape(1, nseq), ratio.reshape(1, nseq),
        q, up, k, v, near, near, far, far,
    )


def add_blocks(ref):
    total = ref[0].astype(F32)
    for i in range(1, ref.shape[0]):
        total = total + ref[i].astype(F32)
    return total


VMEM = pl.BlockSpec(memory_space=pltpu.VMEM)
SMEM = pl.BlockSpec(memory_space=pltpu.SMEM)


def small_call(kernel, name, outs, *args, flops=0, scratch=()):
    size = sum(a.size * a.dtype.itemsize for a in args)
    size += sum(o.size * jnp.dtype(o.dtype).itemsize for o in outs)
    return pl.pallas_call(
        kernel,
        in_specs=[SMEM if a.dtype == jnp.int32 else VMEM for a in args],
        out_specs=[VMEM for _ in outs],
        out_shape=outs,
        scratch_shapes=list(scratch),
        compiler_params=pltpu.CompilerParams(vmem_limit_bytes=32 * 1024 * 1024),
        cost_estimate=pl.CostEstimate(flops=flops, bytes_accessed=size, transcendentals=0),
        name=name,
    )(*args)


def bf16(*shape):
    return jax.ShapeDtypeStruct(shape, BF16)


def message_kernel(groups, nz, rows_out, keys, values, hidden, out):
    slots, width = keys.shape
    chunk = hidden.shape[1] // groups
    pieces = [hidden[:, i * chunk : (i + 1) * chunk].astype(F32) for i in range(groups)]
    if groups * slots < HD:
        pieces.append(jnp.zeros((HD - groups * slots, chunk), F32))
    stacked = jnp.concatenate(pieces, axis=0).astype(BF16)
    row = lax.broadcasted_iota(jnp.int32, (nz * CORES * SUB, chunk), 0)
    column = lax.broadcasted_iota(jnp.int32, (nz * CORES * SUB, chunk), 1)
    item = row % SUB
    picks = (column == (row // SUB) * rows_out + item) & (item < rows_out)
    turned = lax.dot_general(
        jnp.where(picks, 1.0, 0.0).astype(BF16),
        stacked,
        (((1,), (1,)), ((), ())),
        preferred_element_type=F32,
    ).reshape(nz, CORES, SUB, HD)
    out[:, 0:width] = jnp.concatenate([keys[...].astype(F32)] * nz, axis=0).astype(BF16)
    out[:, width : 2 * width] = jnp.concatenate([values[...].astype(F32)] * nz, axis=0).astype(BF16)
    for core in range(CORES):
        lo = 2 * width + core * HD
        out[:, lo : lo + HD] = turned[:, core].reshape(nz * SUB, HD).astype(BF16)


def message(keys, values, hidden, groups, nz, rows_out):
    slots, width = keys.shape
    return small_call(
        functools.partial(message_kernel, groups, nz, rows_out), "message",
        [bf16(nz * slots, 2 * width + CORES * HD)], keys, values, hidden,
    )[0]


def turn_kernel(groups, nzh, nzl, got, out):
    count = groups * CORES * SUB
    lanes = CORES * HD
    slots = SUB
    row = lax.broadcasted_iota(jnp.int32, (count, lanes), 0)
    lane = lax.broadcasted_iota(jnp.int32, (count, lanes), 1)
    mine = ((lane // HD) == (row // SUB) % CORES) & (((lane % HD) // slots) == row // (SUB * CORES))
    from_lane = lax.broadcasted_iota(jnp.int32, (lanes, nzh * nzl * slots), 0)
    to_lane = lax.broadcasted_iota(jnp.int32, (lanes, nzh * nzl * slots), 1)
    total = jnp.zeros((count, nzh * nzl * slots), F32)
    for zh in range(nzh):
        for zl in range(nzl):
            z = zh * nzl + zl
            block = got[z * SUB : (z + 1) * SUB, :].astype(F32)
            block = jnp.where(mine, jnp.concatenate([block] * (count // SUB), axis=0), 0.0)
            place = to_lane == (zl * nzh + zh) * slots + from_lane % slots
            total = total + jnp.dot(
                block.astype(BF16),
                jnp.where(place, 1.0, 0.0).astype(BF16),
                preferred_element_type=F32,
            )
    out[...] = total.astype(BF16)


def turn(got, groups, nzh, nzl):
    shape = bf16(groups * CORES * SUB, nzh * nzl * SUB)
    return small_call(functools.partial(turn_kernel, groups, nzh, nzl), "turn", [shape], got)[0]


def merge_kernel(keep, got, out):
    width = keep.shape[2]
    out[:, 0:width] = (keep[0] + got[0].astype(F32)).astype(BF16)
    out[:, width:] = (keep[1] + got[1].astype(F32)).astype(BF16)


def merge(keep, got):
    _, rows, width = keep.shape
    return small_call(merge_kernel, "merge", [bf16(rows, 2 * width)], keep, got)[0]


def zh_kernel(slots, got, out):
    total = add_blocks(got)
    rows = total.shape[0]
    width = total.shape[1] // 2
    keys = total[:, 0:width].astype(BF16)
    for zh in range(out.shape[0]):
        own = total[zh * slots : (zh + 1) * slots, width:]
        out[zh, 0:rows, :] = keys
        out[zh, rows:, :] = jnp.concatenate([own, jnp.zeros_like(own)], axis=0).astype(BF16)


def zh_message(got, nzh, slots):
    _, rows, lanes = got.shape
    shape = bf16(nzh, rows + 2 * slots, lanes // 2)
    return small_call(functools.partial(zh_kernel, slots), "zh_message", [shape], got)[0]


def owner_kernel(slots, rows, place, got, keys, values, spread, total):
    total[...] = add_blocks(got)
    first = pl.multiple_of(place[1] * slots, slots)
    keys[...] = total[pl.ds(first, slots), :].astype(BF16)
    values[...] = total[rows : rows + slots, :].astype(BF16)
    every = total[0:rows, :].astype(BF16)
    for zl in range(spread.shape[0]):
        spread[zl] = every


def owner_rows(place, got, nzl, slots):
    nzh, tall, width = got.shape
    rows = nzh * slots
    return small_call(
        functools.partial(owner_kernel, slots, rows), "owner_rows",
        [bf16(slots, width), bf16(slots, width), bf16(nzl, rows, width)], place, got,
        scratch=[pltpu.VMEM((tall, width), F32)],
    )


def weight_kernel(hidden, keys, out):
    out[...] = jnp.dot(hidden[...], keys[...], preferred_element_type=F32).astype(BF16)


def weight_terms(hidden, keys):
    rows, width = keys.shape
    count = hidden.shape[0]
    return small_call(
        weight_kernel, "weight_terms", [bf16(count, width)], hidden, keys,
        flops=2 * count * rows * width,
    )[0]


def per_device(
    nx, nzh, nzl,
    queries, keys, values, grad_out, beacon_keys, beacon_values, beacon_hidden, order, ratio,
):
    ndp = lax.axis_size("dp")
    nz = nzh * nzl
    slots, width = beacon_keys.shape[1:]
    model = beacon_hidden.shape[2]
    groups = ndp * nx
    rows_out = model // (groups * nz * CORES)
    half = nx * nz * slots
    swap = [(0, 1), (1, 0)]
    zh, zl = lax.axis_index("zh"), lax.axis_index("zl")
    place = [lax.axis_index("x"), zh * nzl + zl, lax.axis_index("core")]
    place = jnp.stack(place).astype(jnp.int32)
    zh_place = jnp.stack([zl, zh]).astype(jnp.int32)

    first = message(beacon_keys[0], beacon_values[0], beacon_hidden[0], groups, nz, rows_out)
    first = lax.all_to_all(first.reshape(nz, slots, -1), ("zh", "zl"), 0, 0, tiled=True)
    near = first[:, :, : 2 * width].reshape(1, nz * slots, 2 * width)
    near = jnp.broadcast_to(near, (nx, nz * slots, 2 * width))
    near = lax.all_to_all(near, "x", 0, 0, tiled=True).reshape(half, 2 * width)
    far = lax.ppermute(near, "core", swap)
    hidden = turn(first[:, :, 2 * width :].reshape(nz * slots, CORES * HD), groups, nzh, nzl)

    dq, dk, dv, keep, send = attention(
        place, order, ratio, queries[0], grad_out[0], keys[0], values[0], near, far,
        nx, nzh, nzl, slots,
    )

    terms = merge(keep, lax.ppermute(send, "core", swap))
    terms = terms.reshape(nx * nzl, nzh * slots, 2 * width)
    terms = lax.all_to_all(terms, ("x", "zl"), 0, 0, tiled=True)
    terms = lax.all_to_all(zh_message(terms, nzh, slots), "zh", 0, 0, tiled=True)
    beacon_dk, beacon_dv, spread = owner_rows(zh_place, terms, nzl, slots)
    spread = lax.all_to_all(spread, "zl", 0, 0, tiled=True).reshape(nz * slots, width)
    weights = weight_terms(hidden, spread).reshape(groups * CORES, SUB, width)
    weights = lax.all_to_all(weights, ("dp", "x", "core"), 0, 0, tiled=True)
    weight_grad = jnp.sum(weights.astype(F32), axis=0)[:rows_out]
    return (dq[None], dk[None], dv[None], beacon_dk[None], beacon_dv[None], weight_grad)


def solution(mesh):
    ndp, nx, nzh, nzl = grid_of(mesh)
    fine = Mesh(
        mesh.devices.reshape(ndp, nx, nzh, nzl, CORES), ("dp", "x", "zh", "zl", "core")
    )
    seq = ("x", "zh", "zl", "core")
    split = P("dp", seq, None)
    return jax.shard_map(
        functools.partial(per_device, nx, nzh, nzl),
        mesh=fine,
        in_specs=(split,) * 7 + (P(), P()),
        out_specs=(split,) * 5 + (P(("dp",) + seq, None),),
        check_vma=False,
    )
```

time: 170 us -> 134 us (0.79)
  the two profiles are of different devices: /device:TPU:2 before, /device:TPU:1 now
where the time goes in v2:
time: 134 us; the launch traced here: 133 us
  blocking collectives  76.2 us (57%)
  starting transfers between devices  19.1 us (14%)
  waiting for transfers between devices  18.8 us (14%)
  Pallas kernels  14.7 us (11%)
  local copies, waits for them, and re-layouts  2.9 us (2%)
    all_to_all x1, blocking collectives, per_device(): lax.all_to_all(first.reshape(nz, slots, -1), ('zh', 'zl'), 0, 0, tiled=True)  28.1 us
    all_to_all x1, blocking collectives, per_device(): terms = lax.all_to_all(terms, ('x', 'zl'), 0, 0, tiled=True)  20 us
    all_to_all x1, blocking collectives, per_device(): weights = lax.all_to_all(weights, ('dp', 'x', 'core'), 0, 0, tiled=True)  17.3 us
    all_to_all x1, waiting for transfers between devices, per_device(): lax.all_to_all(zh_message(terms, nzh, slots), 'zh', 0, 0, tiled=True)  12.1 us
    pallas_call x1, Pallas kernels, attention(): pl.pallas_call(functools.partial(attention_kernel, nx, nzh, nzl, slots, s...  11.4 us
    all_to_all x1, blocking collectives, per_device(): near = lax.all_to_all(near, 'x', 0, 0, tiled=True).reshape(half, 2 * width)  10.9 us
    ppermute x1, starting transfers between devices, per_device(): far = lax.ppermute(near, 'core', swap)  8.16 us
    all_to_all x1, starting transfers between devices, per_device(): lax.all_to_all(zh_message(terms, nzh, slots), 'zh', 0, 0, tiled=True)  5.44 us
  transfers between devices with their start and end apart: 4, of which 4 were waited for; matrix products, arithmetic and copies ran while one was open for 0% of the time, Pallas kernels for 1%

profile of v2, /device:TPU:1, one launch (start us, length us, event | category | flops | bytes accessed | tf_op | source)
XLA Modules:
  0.0 133.3 jit_solution(8962545979807441081)
XLA Ops:
  0.6 0.0 copy-start.1
  0.6 0.7 copy-done.1
  1.3 0.0 copy-start
  1.3 0.8 copy-done
  2.1 0.0 copy-start.2
  2.1 0.7 copy-done.2
  2.8 0.3 message.1
  3.1 28.1 %all_to_all.30 = bf16[16,8,768]{2,1,0:T(8,128)(2,1)S(1)} all-to-all(bf16[16,8,768]{2,1,0:T(8,128)(2,1)S(1)} %bitcast.30), channel_id=1, replica_groups=mesh['dp'=4,'x'=4,'zh'=4,'zl'=4,'core'=2] {'zh','zl'}, dimensions={0} | all-to-all | bytes 393216 | tf_op jit(solution)/shard_map/all_to_all | solution.py:337
  31.2 0.0 copy-start.3
  31.3 0.0 copy-start.4
  31.3 0.0 copy-start.5
  31.3 0.0 copy-start.6
  31.3 10.9 %all_to_all.31 = bf16[4,128,512]{2,1,0:T(8,128)(2,1)S(1)} all-to-all(bf16[4,128,512]{2,1,0:T(8,128)(2,1)S(1)} %broadcast_in_dim.23), channel_id=1, replica_groups=mesh['dp'=4,'x'=4,'zh'=4,'zl'=4,'core'=2] {'x'}, dimensions={0} | all-to-all | bytes 1048576 | tf_op jit(solution)/shard_map/all_to_all | solution.py:340
  42.2 8.2 %collective-permute-start = (bf16[512,512]{1,0:T(8,128)(2,1)S(1)}, bf16[512,512]{1,0:T(8,128)(2,1)S(1)}, u32[]{:S(2)}, u32[]{:S(2)}) collective-permute-start(bf16[512,512]{1,0:T(8,128)(2,1)S(1)} %bitcast.31), channel_id=1, source_target_pairs={{0,1},{1,0},{2,3},{3,2},{4,5},{5,4},{6,7},{7,6},{8,9},{9,8},{10,11... | collective-permute-start | bytes 1572872 | tf_op jit(solution)/shard_map/ppermute | solution.py:341
  50.4 0.1 pad_add_fusion.place
  50.4 1.4 %collective-permute-done.far_k.far_v = bf16[512,512]{1,0:T(8,128)(2,1)S(1)} collective-permute-done((bf16[512,512]{1,0:T(8,128)(2,1)S(1)}, bf16[512,512]{1,0:T(8,128)(2,1)S(1)}, u32[]{:S(2)}, u32[]{:S(2)}) %collective-permute-start) | collective-permute-done | bytes 524320 | tf_op jit(solution)/shard_map/ppermute | solution.py:341
  51.9 0.0 copy-start.7
  51.9 0.0 copy-start.8
  51.9 0.0 copy-done.3
  51.9 0.0 copy-done.4
  51.9 0.0 copy-done.5
  51.9 0.0 copy-done.6
  51.9 0.6 copy-done.7
  52.5 0.0 copy-done.8
  52.5 11.4 %attention.1 = (bf16[128,1792]{1,0:T(8,128)(2,1)}, bf16[128,256]{1,0:T(8,128)(2,1)}, bf16[128,256]{1,0:T(8,128)(2,1)}, f32[2,512,256]{2,1,0:T(8,128)S(1)}, bf16[2,512,256]{2,1,0:T(8,128)(2,1)S(1)}) custom-call(s32[3]{0:T(128)S(1)} %pad_add_fusion.place, s32[128]{0:T(128)S(1)} %copy-done.7, s32[1,128]{1,0:T(1,128)S(1)} %bitcast.43, s32[1,128]{1,0:T(1,128)S(1)} %bitcast.44, ...), custom_call_target="tpu_custom_call" | custom-call | flops 2642411520 | bytes 4194304 | tf_op jit(solution)/shard_map/attention/pallas_call | solution.py:132
  64.0 2.3 %collective-permute-start.1 = (bf16[2,512,256]{2,1,0:T(8,128)(2,1)S(1)}, bf16[2,512,256]{2,1,0:T(8,128)(2,1)S(1)}, u32[]{:S(2)}, u32[]{:S(2)}) collective-permute-start(bf16[2,512,256]{2,1,0:T(8,128)(2,1)S(1)} %get-tuple-element.18), channel_id=1, source_target_pairs={{0,1},{1,0},{2,3},{3,2},{4,5},{5,4},{6,7},{7,6},{8,9},{9,8},{10,11... | collective-permute-start | bytes 1572872 | tf_op jit(solution)/shard_map/ppermute | solution.py:349
  66.2 1.5 %collective-permute-done.1.got = bf16[2,512,256]{2,1,0:T(8,128)(2,1)S(1)} collective-permute-done((bf16[2,512,256]{2,1,0:T(8,128)(2,1)S(1)}, bf16[2,512,256]{2,1,0:T(8,128)(2,1)S(1)}, u32[]{:S(2)}, u32[]{:S(2)}) %collective-permute-start.1) | collective-permute-done | bytes 524320 | tf_op jit(solution)/shard_map/ppermute | solution.py:349
  67.8 0.1 merge.1
  67.9 20.0 %all_to_all.32.got = bf16[16,32,512]{2,1,0:T(8,128)(2,1)S(1)} all-to-all(bf16[16,32,512]{2,1,0:T(8,128)(2,1)S(1)} %bitcast.29), channel_id=1, replica_groups=mesh['dp'=4,'x'=4,'zh'=4,'zl'=4,'core'=2] {'x','zl'}, dimensions={0} | all-to-all | bytes 1048576 | tf_op jit(solution)/shard_map/all_to_all | solution.py:351
  87.9 0.7 zh_message.1
  88.6 5.4 %all-to-all-start.3 = ((bf16[4,48,256]{2,1,0:T(8,128)(2,1)}), bf16[4,48,256]{2,1,0:T(8,128)(2,1)S(1)}, u32[]{:S(2)}, u32[]{:S(2)}) async-start(bf16[4,48,256]{2,1,0:T(8,128)(2,1)} %zh_message.1), calls=%async_computation.3 | async-start | bytes 196608 | tf_op jit(solution)/shard_map/all_to_all | solution.py:352
  94.0 0.1 pad_add_fusion.1.place
  94.1 12.1 %all-to-all-done.3.got = bf16[4,48,256]{2,1,0:T(8,128)(2,1)S(1)} async-done(((bf16[4,48,256]{2,1,0:T(8,128)(2,1)}), bf16[4,48,256]{2,1,0:T(8,128)(2,1)S(1)}, u32[]{:S(2)}, u32[]{:S(2)}) %all-to-all-start.3) | async-done | bytes 98336 | tf_op jit(solution)/shard_map/all_to_all | solution.py:352
  106.2 1.2 owner_rows.1
  107.3 3.3 %all-to-all-start.4 = ((bf16[4,32,256]{2,1,0:T(8,128)(2,1)}), bf16[4,32,256]{2,1,0:T(8,128)(2,1)S(1)}, u32[]{:S(2)}, u32[]{:S(2)}) async-start(bf16[4,32,256]{2,1,0:T(8,128)(2,1)} %get-tuple-element.21), calls=%async_computation.4 | async-start | bytes 131072 | tf_op jit(solution)/shard_map/all_to_all | solution.py:354
  110.6 0.8 turn.1.hidden
  111.5 3.7 %all-to-all-done.4 = bf16[4,32,256]{2,1,0:T(8,128)(2,1)S(1)} async-done(((bf16[4,32,256]{2,1,0:T(8,128)(2,1)}), bf16[4,32,256]{2,1,0:T(8,128)(2,1)S(1)}, u32[]{:S(2)}, u32[]{:S(2)}) %all-to-all-start.4) | async-done | bytes 65568 | tf_op jit(solution)/shard_map/all_to_all | solution.py:354
  115.2 0.2 weight_terms.1
  115.4 17.3 %all_to_all.33 = bf16[32,8,256]{2,1,0:T(8,128)(2,1)S(1)} all-to-all(bf16[32,8,256]{2,1,0:T(8,128)(2,1)S(1)} %bitcast.34), channel_id=1, replica_groups=mesh['dp'=4,'x'=4,'zh'=4,'zl'=4,'core'=2] {'dp','x','core'}, dimensions={0} | all-to-all | bytes 262144 | tf_op jit(solution)/shard_map/all_to_all | solution.py:356
  132.6 0.6 convert_reduce_fusion
  (3 shorter events, 0.1 us)
Async XLA Ops:
  0.6 0.7 copy-start.1
  1.3 0.8 copy-start
  2.1 0.7 copy-start.2
  31.2 20.6 %copy-start.3 = (bf16[1,128,1792]{2,1,0:T(8,128)(2,1)S(1)}, bf16[1,128,1792]{2,1,0:T(8,128)(2,1)}, u32[]{:S(2)}) copy-start(bf16[1,128,1792]{2,1,0:T(8,128)(2,1)} %param.9) | copy-start | bytes 1376260
  31.3 20.6 %copy-start.4 = (bf16[1,128,1792]{2,1,0:T(8,128)(2,1)S(1)}, bf16[1,128,1792]{2,1,0:T(8,128)(2,1)}, u32[]{:S(2)}) copy-start(bf16[1,128,1792]{2,1,0:T(8,128)(2,1)} %param.12) | copy-start | bytes 1376260
  31.3 20.6 %copy-start.5 = (bf16[1,128,256]{2,1,0:T(8,128)(2,1)S(1)}, bf16[1,128,256]{2,1,0:T(8,128)(2,1)}, u32[]{:S(2)}) copy-start(bf16[1,128,256]{2,1,0:T(8,128)(2,1)} %param.10) | copy-start | bytes 196612
  31.3 20.6 %copy-start.6 = (bf16[1,128,256]{2,1,0:T(8,128)(2,1)S(1)}, bf16[1,128,256]{2,1,0:T(8,128)(2,1)}, u32[]{:S(2)}) copy-start(bf16[1,128,256]{2,1,0:T(8,128)(2,1)} %param.11) | copy-start | bytes 196612
  42.2 9.7 %collective-permute-start = (bf16[512,512]{1,0:T(8,128)(2,1)S(1)}, bf16[512,512]{1,0:T(8,128)(2,1)S(1)}, u32[]{:S(2)}, u32[]{:S(2)}) collective-permute-start(bf16[512,512]{1,0:T(8,128)(2,1)S(1)} %bitcast.31), channel_id=1, source_target_pairs={{0,1},{1,0},{2,3},{3,2},{4,5},{5,4},{6,7},{7,6},{8,9},{9,8},{10,11... | collective-permute-start | bytes 1572872 | tf_op jit(solution)/shard_map/ppermute | solution.py:341
  51.9 0.7 copy-start.7
  51.9 0.7 copy-start.8
  64.0 3.8 %collective-permute-start.1 = (bf16[2,512,256]{2,1,0:T(8,128)(2,1)S(1)}, bf16[2,512,256]{2,1,0:T(8,128)(2,1)S(1)}, u32[]{:S(2)}, u32[]{:S(2)}) collective-permute-start(bf16[2,512,256]{2,1,0:T(8,128)(2,1)S(1)} %get-tuple-element.18), channel_id=1, source_target_pairs={{0,1},{1,0},{2,3},{3,2},{4,5},{5,4},{6,7},{7,6},{8,9},{9,8},{10,11... | collective-permute-start | bytes 1572872 | tf_op jit(solution)/shard_map/ppermute | solution.py:349
  88.6 17.6 %all-to-all-start.3 = ((bf16[4,48,256]{2,1,0:T(8,128)(2,1)}), bf16[4,48,256]{2,1,0:T(8,128)(2,1)S(1)}, u32[]{:S(2)}, u32[]{:S(2)}) async-start(bf16[4,48,256]{2,1,0:T(8,128)(2,1)} %zh_message.1), calls=%async_computation.3 | async-start | bytes 196608 | tf_op jit(solution)/shard_map/all_to_all | solution.py:352
  107.3 7.9 %all-to-all-start.4 = ((bf16[4,32,256]{2,1,0:T(8,128)(2,1)}), bf16[4,32,256]{2,1,0:T(8,128)(2,1)S(1)}, u32[]{:S(2)}, u32[]{:S(2)}) async-start(bf16[4,32,256]{2,1,0:T(8,128)(2,1)} %get-tuple-element.21), calls=%async_computation.4 | async-start | bytes 131072 | tf_op jit(solution)/shard_map/all_to_all | solution.py:354

commit v3 on v2

v3 whole, which is shorter than its diff:
```python
import functools
import math

import jax
import jax.numpy as jnp
from jax import lax
from jax.experimental import pallas as pl
from jax.experimental.pallas import tpu as pltpu
from jax.sharding import Mesh
from jax.sharding import PartitionSpec as P

QH = 14
KVH = 2
HD = 128
GROUPS = QH // KVH
NEG = -1e30
SCALE = 1.0 / math.sqrt(HD)
LOG2E = math.log2(math.e)
CORES = 2
SUB = 8
HEADS = 4
F32 = jnp.float32
BF16 = jnp.bfloat16


def grid_of(mesh):
    dp, seq = mesh.devices.shape
    nx, nzl = (4, 4) if seq == 128 else (2, 2)
    return dp, nx, seq // (nx * nzl * CORES), nzl


def visible_bias(order_row, ratio_row, mine, slots, span):
    nseq = order_row.shape[1]
    t = lax.broadcasted_iota(jnp.int32, (nseq, nseq), 0)
    picks = jnp.where(order_row == t, 1.0, 0.0).astype(F32)
    rates = jnp.broadcast_to(ratio_row.astype(F32), (slots, nseq))
    rate = jnp.dot(rates, picks, preferred_element_type=F32)
    cost = jnp.where(order_row < mine, rate, 4.0 * span)
    slot = lax.broadcasted_iota(jnp.int32, (slots, nseq), 0)
    return jnp.where((slot + 1).astype(F32) * cost <= float(span), 0.0, NEG)


def attention_kernel(
    nx, nzh, nzl, slots,
    bias, mine, other, beacons,
    own_out, other_out, terms,
    kcat, vcat, qcat, ucat, probs, dscores,
):
    span = mine.shape[0]
    wide = GROUPS * HD
    sides = (mine, other)
    for r, side in enumerate(sides):
        kcat[r, 0:span, :] = side[:, 2 * wide : 2 * wide + HD]
        vcat[r, 0:span, :] = side[:, 2 * wide + HD :]
        kcat[r, span:, :] = beacons[:, 0:HD]
        vcat[r, span:, :] = beacons[:, HD:]
        for h in range(GROUPS):
            at = (r * GROUPS + h) * span
            qcat[at : at + span, :] = side[:, h * HD : (h + 1) * HD]
            ucat[at : at + span, :] = side[:, wide + h * HD : wide + (h + 1) * HD]

    key_row = lax.broadcasted_iota(jnp.int32, (span, span), 0)
    query_col = lax.broadcasted_iota(jnp.int32, (span, span), 1)
    causal = key_row <= query_col
    contract_last = (((1,), (1,)), ((), ()))
    contract_first = (((0,), (0,)), ((), ()))

    for r in range(CORES):
        for h0 in range(0, GROUPS, HEADS):
            heads = min(HEADS, GROUPS - h0)
            lo = (r * GROUPS + h0) * span
            rows = slice(lo, lo + heads * span)
            s = lax.dot_general(
                kcat[r], qcat[rows, :], contract_last, preferred_element_type=F32
            )
            dp = lax.dot_general(
                vcat[r], ucat[rows, :], contract_last, preferred_element_type=F32
            )
            s = s * (SCALE * LOG2E)
            own = jnp.where(jnp.concatenate([causal] * heads, axis=1), s[0:span, :], NEG)
            far = s[span:, :] + jnp.concatenate([bias[r]] * heads, axis=1)
            s = jnp.concatenate([own, far], axis=0)
            top = jnp.max(s, axis=0, keepdims=True)
            e = jnp.exp2(s - top)
            inv = 1.0 / jnp.sum(e, axis=0, keepdims=True)
            delta = jnp.sum(e * dp, axis=0, keepdims=True) * inv
            p = e * inv
            probs[:, rows] = p.astype(BF16)
            dscores[:, rows] = (p * (dp - delta)).astype(BF16)

    products = ((0, dscores, qcat, SCALE), (1, probs, ucat, 1.0))
    for kind, left, right, scale in products:
        full = jnp.dot(left[span:, :], right[...], preferred_element_type=F32) * scale
        count = full.shape[0]
        full = full.reshape(nx, nzh, nzl, CORES * slots, HD)
        full = jnp.swapaxes(full, 1, 2).reshape(count, HD)
        terms[:, kind * HD : (kind + 1) * HD] = full.astype(BF16)
    for r, out in enumerate((own_out, other_out)):
        rows = slice(r * wide, (r + 1) * wide)
        for kind, left, right, scale in products:
            part = jnp.dot(left[0:span, rows], right[rows, :], preferred_element_type=F32)
            lo = wide + kind * HD
            out[:, lo : lo + HD] = (part * scale).astype(BF16)
        part = lax.dot_general(
            kcat[r], dscores[:, rows], contract_first, preferred_element_type=F32
        ) * SCALE
        for h in range(GROUPS):
            lanes = slice(h * HD, (h + 1) * HD)
            out[:, lanes] = part[:, h * span : (h + 1) * span].T.astype(BF16)


def attention(bias, mine, other, beacons, nx, nzh, nzl, slots):
    span = mine.shape[0]
    total, lanes = beacons.shape
    keys = span + total
    wide = GROUPS * HD
    return small_call(
        functools.partial(attention_kernel, nx, nzh, nzl, slots), "attention",
        [bf16(span, wide + lanes), bf16(span, wide + lanes), bf16(total, lanes)],
        bias, mine, other, beacons,
        flops=5 * 2 * QH * span * keys * HD,
        scratch=[
            pltpu.VMEM((CORES, keys, HD), BF16),
            pltpu.VMEM((CORES, keys, HD), BF16),
            pltpu.VMEM((CORES * wide, HD), BF16),
            pltpu.VMEM((CORES * wide, HD), BF16),
            pltpu.VMEM((keys, CORES * wide), BF16),
            pltpu.VMEM((keys, CORES * wide), BF16),
        ],
    )


def add_blocks(ref):
    total = ref[0].astype(F32)
    for i in range(1, ref.shape[0]):
        total = total + ref[i].astype(F32)
    return total


VMEM = pl.BlockSpec(memory_space=pltpu.VMEM)
SMEM = pl.BlockSpec(memory_space=pltpu.SMEM)


def small_call(kernel, name, outs, *args, flops=0, scratch=()):
    size = sum(a.size * a.dtype.itemsize for a in args)
    size += sum(o.size * jnp.dtype(o.dtype).itemsize for o in outs)
    return pl.pallas_call(
        kernel,
        in_specs=[SMEM if a.dtype == jnp.int32 else VMEM for a in args],
        out_specs=[VMEM for _ in outs],
        out_shape=outs,
        scratch_shapes=list(scratch),
        compiler_params=pltpu.CompilerParams(vmem_limit_bytes=48 * 1024 * 1024),
        cost_estimate=pl.CostEstimate(flops=flops, bytes_accessed=size, transcendentals=0),
        name=name,
    )(*args)


def bf16(*shape):
    return jax.ShapeDtypeStruct(shape, BF16)


def message_kernel(groups, nz, rows_out, keys_in, values_in, hidden_in, out, keys, values, hidden, sems):
    copies = [
        pltpu.make_async_copy(source, held, sems.at[i])
        for i, (source, held) in enumerate(
            ((hidden_in, hidden), (keys_in, keys), (values_in, values))
        )
    ]
    for copy in copies:
        copy.start()
    for copy in copies:
        copy.wait()
    slots, width = keys.shape
    chunk = hidden.shape[1] // groups
    pieces = [hidden[:, i * chunk : (i + 1) * chunk].astype(F32) for i in range(groups)]
    if groups * slots < HD:
        pieces.append(jnp.zeros((HD - groups * slots, chunk), F32))
    stacked = jnp.concatenate(pieces, axis=0).astype(BF16)
    row = lax.broadcasted_iota(jnp.int32, (nz * CORES * SUB, chunk), 0)
    column = lax.broadcasted_iota(jnp.int32, (nz * CORES * SUB, chunk), 1)
    item = row % SUB
    picks = (column == (row // SUB) * rows_out + item) & (item < rows_out)
    turned = lax.dot_general(
        jnp.where(picks, 1.0, 0.0).astype(BF16),
        stacked,
        (((1,), (1,)), ((), ())),
        preferred_element_type=F32,
    )
    both = []
    for core in range(CORES):
        lanes = slice(core * HD, (core + 1) * HD)
        both.append(jnp.concatenate([keys[:, lanes], values[:, lanes]], axis=1).astype(F32))
    out[:, 0:width] = jnp.concatenate(both * nz, axis=0).astype(BF16)
    out[:, width:] = turned.astype(BF16)


def message(keys, values, hidden, groups, nz, rows_out):
    slots, width = keys.shape
    anywhere = pl.BlockSpec(memory_space=pl.ANY)
    return pl.pallas_call(
        functools.partial(message_kernel, groups, nz, rows_out),
        in_specs=[anywhere] * 3,
        out_specs=VMEM,
        out_shape=bf16(nz * CORES * slots, width + HD),
        scratch_shapes=[
            *[pltpu.VMEM(a.shape, BF16) for a in (keys, values, hidden)],
            pltpu.SemaphoreType.DMA((3,)),
        ],
        compiler_params=pltpu.CompilerParams(vmem_limit_bytes=56 * 1024 * 1024),
        cost_estimate=pl.CostEstimate(
            flops=0, bytes_accessed=512 * 1024, transcendentals=0
        ),
        name="message",
    )(keys, values, hidden)


def split_kernel(place, q, up, k, v, mine, send):
    wide = GROUPS * HD
    core = place[2]
    for out, head in ((mine, core), (send, 1 - core)):
        lanes = pl.ds(pl.multiple_of(head * wide, HD), wide)
        out[:, 0:wide] = q[:, lanes]
        out[:, wide : 2 * wide] = up[:, lanes]
        lanes = pl.ds(pl.multiple_of(head * HD, HD), HD)
        out[:, 2 * wide : 2 * wide + HD] = k[:, lanes]
        out[:, 2 * wide + HD :] = v[:, lanes]


def split_heads(place, q, up, k, v):
    shape = bf16(q.shape[0], 2 * GROUPS * HD + 2 * HD)
    return small_call(split_kernel, "split_heads", [shape, shape], place, q, up, k, v)


def join_kernel(place, mine, got, dq, dk, dv):
    wide = GROUPS * HD
    core = place[2]
    for part, head in ((mine, core), (got, 1 - core)):
        dq[:, pl.ds(pl.multiple_of(head * wide, HD), wide)] = part[:, 0:wide]
        lanes = pl.ds(pl.multiple_of(head * HD, HD), HD)
        dk[:, lanes] = part[:, wide : wide + HD]
        dv[:, lanes] = part[:, wide + HD :]


def join_heads(place, mine, got):
    span = mine.shape[0]
    shapes = [bf16(span, QH * HD), bf16(span, KVH * HD), bf16(span, KVH * HD)]
    return small_call(join_kernel, "join_heads", shapes, place, mine, got)


def mask_kernel(nz, slots, span, place, order_s, order_row, ratio_row, bias):
    core = place[2]
    first = (place[0] * nz + place[1]) * CORES
    for r, index in enumerate((first + core, first + 1 - core)):
        owners = visible_bias(order_row[...], ratio_row[...], order_s[index], slots, span)
        for j in range(owners.shape[1]):
            tile = jnp.broadcast_to(owners[:, j : j + 1], (slots, HD))
            bias[r, j * slots : (j + 1) * slots, :] = tile


def mask(place, order, ratio, nz, slots, span):
    nseq = order.shape[0]
    return pl.pallas_call(
        functools.partial(mask_kernel, nz, slots, span),
        in_specs=[SMEM, SMEM, VMEM, VMEM],
        out_specs=VMEM,
        out_shape=jax.ShapeDtypeStruct((CORES, nseq * slots, HD), F32),
        compiler_params=pltpu.CompilerParams(vmem_limit_bytes=32 * 1024 * 1024),
        cost_estimate=pl.CostEstimate(
            flops=0, bytes_accessed=2 * 1024 * 1024, transcendentals=0
        ),
        name="mask",
    )(place, order, order.reshape(1, nseq), ratio.reshape(1, nseq))


def turn_kernel(groups, nzh, nzl, slots, got, out):
    count = groups * SUB
    width = nzh * nzl * CORES * slots
    row = lax.broadcasted_iota(jnp.int32, (count, HD), 0)
    lane = lax.broadcasted_iota(jnp.int32, (count, HD), 1)
    same = lane // slots == row // SUB
    from_lane = lax.broadcasted_iota(jnp.int32, (HD, width), 0)
    to_lane = lax.broadcasted_iota(jnp.int32, (HD, width), 1)
    total = jnp.zeros((count, width), F32)
    for zh in range(nzh):
        for zl in range(nzl):
            for c in range(CORES):
                source = (zh * nzl + zl) * CORES + c
                target = (zl * nzh + zh) * CORES + c
                block = got[source * SUB : (source + 1) * SUB, :].astype(F32)
                block = jnp.where(same, jnp.concatenate([block] * groups, axis=0), 0.0)
                put = to_lane == target * slots + from_lane % slots
                total = total + jnp.dot(
                    block.astype(BF16),
                    jnp.where(put, 1.0, 0.0).astype(BF16),
                    preferred_element_type=F32,
                )
    out[...] = total.astype(BF16)


def turn(got, groups, nzh, nzl, slots):
    shape = bf16(groups * SUB, nzh * nzl * CORES * slots)
    kernel = functools.partial(turn_kernel, groups, nzh, nzl, slots)
    return small_call(kernel, "turn", [shape], got)[0]


def zh_kernel(got, out):
    total = add_blocks(got)
    rows = total.shape[0]
    each = rows // out.shape[0]
    keys = total[:, 0:HD].astype(BF16)
    for zh in range(out.shape[0]):
        out[zh, 0:rows, :] = keys
        out[zh, rows:, :] = total[zh * each : (zh + 1) * each, HD:].astype(BF16)


def zh_message(got, nzh):
    _, rows, _ = got.shape
    return small_call(zh_kernel, "zh_message", [bf16(nzh, rows + rows // nzh, HD)], got)[0]


def spread_kernel(got, out):
    total = add_blocks(got).astype(BF16)
    for i in range(out.shape[0]):
        out[i] = total


def spread(got, peers):
    return small_call(spread_kernel, "spread", [bf16(peers, *got.shape[1:])], got)[0]


def weight_kernel(rows, hidden, got, out):
    pairs = []
    for zl in range(got.shape[0] // CORES):
        heads = [got[zl * CORES + c, 0:rows, :] for c in range(CORES)]
        pairs.append(jnp.concatenate(heads, axis=1))
    keys = jnp.concatenate(pairs, axis=0)
    out[...] = jnp.dot(hidden[...], keys, preferred_element_type=F32).astype(BF16)


def weight_terms(hidden, got, rows):
    count, depth = hidden.shape
    return small_call(
        functools.partial(weight_kernel, rows), "weight_terms", [bf16(count, CORES * HD)],
        hidden, got, flops=2 * count * depth * CORES * HD,
    )[0]


def finish_kernel(nzl, slots, rows, place, got, weights, keys, values, weight_grad, held):
    zh, zl = place[1] // nzl, place[1] % nzl
    core = place[2]
    key_row = pl.multiple_of((zh * CORES + core) * slots, slots)
    value_row = pl.multiple_of(rows + core * slots, slots)
    for c in range(CORES):
        held[c] = got[pl.ds(zl * CORES + c, 1)][0].astype(F32)
        lanes = slice(c * HD, (c + 1) * HD)
        keys[:, lanes] = held[c, pl.ds(key_row, slots), :].astype(BF16)
        values[:, lanes] = held[c, pl.ds(value_row, slots), :].astype(BF16)
    weight_grad[...] = add_blocks(weights)[0 : weight_grad.shape[0], :]


def finish(place, got, weights, nzl, slots, rows, rows_out):
    width = weights.shape[2]
    return small_call(
        functools.partial(finish_kernel, nzl, slots, rows), "finish",
        [
            bf16(slots, width),
            bf16(slots, width),
            jax.ShapeDtypeStruct((rows_out, width), F32),
        ],
        place, got, weights, scratch=[pltpu.VMEM((CORES, *got.shape[1:]), F32)],
    )


def per_device(
    nx, nzh, nzl,
    queries, keys, values, grad_out, beacon_keys, beacon_values, beacon_hidden, order, ratio,
):
    ndp = lax.axis_size("dp")
    nz = nzh * nzl
    span = queries.shape[1]
    slots, width = beacon_keys.shape[1:]
    model = beacon_hidden.shape[2]
    groups = ndp * nx
    rows_out = model // (groups * nz * CORES)
    swap = [(0, 1), (1, 0)]
    z_index = lax.axis_index("zh") * nzl + lax.axis_index("zl")
    place = jnp.stack([lax.axis_index("x"), z_index, lax.axis_index("core")]).astype(jnp.int32)

    first = message(beacon_keys[0], beacon_values[0], beacon_hidden[0], groups, nz, rows_out)
    first = first.reshape(nz * CORES, slots, width + HD)
    first = lax.all_to_all(first, ("zh", "zl", "core"), 0, 0, tiled=True)
    mine, send = split_heads(place, queries[0], grad_out[0], keys[0], values[0])
    other = lax.ppermute(send, "core", swap)
    bias = mask(place, order, ratio, nz, slots, span)
    first, mine, other, bias = lax.optimization_barrier((first, mine, other, bias))

    beacons = first[:, :, :width].reshape(1, nz * CORES * slots, width)
    beacons = jnp.broadcast_to(beacons, (nx, nz * CORES * slots, width))
    beacons = lax.all_to_all(beacons, "x", 0, 0, tiled=True)
    beacons = beacons.reshape(nx * nz * CORES * slots, width)

    own_out, other_out, terms = attention(bias, mine, other, beacons, nx, nzh, nzl, slots)

    terms = terms.reshape(nx * nzl, nzh * CORES * slots, width)
    terms = lax.all_to_all(terms, ("x", "zl"), 0, 0, tiled=True)
    dq, dk, dv = join_heads(place, own_out, lax.ppermute(other_out, "core", swap))
    hidden = first[:, :, width:].reshape(nz * CORES * slots, HD)
    hidden = turn(hidden, groups, nzh, nzl, slots)
    terms, hidden, dq, dk, dv = lax.optimization_barrier((terms, hidden, dq, dk, dv))

    terms = lax.all_to_all(zh_message(terms, nzh), "zh", 0, 0, tiled=True)
    terms = lax.all_to_all(spread(terms, nzl * CORES), ("zl", "core"), 0, 0, tiled=True)
    depth = nzh * CORES * slots
    weights = weight_terms(hidden, terms, depth).reshape(groups, SUB, width)
    weights = lax.all_to_all(weights, ("dp", "x"), 0, 0, tiled=True)
    beacon_dk, beacon_dv, weight_grad = finish(place, terms, weights, nzl, slots, depth, rows_out)
    return (dq[None], dk[None], dv[None], beacon_dk[None], beacon_dv[None], weight_grad)


def solution(mesh):
    ndp, nx, nzh, nzl = grid_of(mesh)
    fine = Mesh(
        mesh.devices.reshape(ndp, nx, nzh, nzl, CORES), ("dp", "x", "zh", "zl", "core")
    )
    seq = ("x", "zh", "zl", "core")
    split = P("dp", seq, None)
    return jax.shard_map(
        functools.partial(per_device, nx, nzh, nzl),
        mesh=fine,
        in_specs=(split,) * 7 + (P(), P()),
        out_specs=(split,) * 5 + (P(("dp",) + seq, None),),
        check_vma=False,
    )
```

time: 134 us -> 120 us (0.90)
  blocking collectives: 76.2 us -> 50.2 us
  starting transfers between devices: 19.1 us -> 27.4 us
  waiting for transfers between devices: 18.8 us -> 22.8 us
  Pallas kernels: 14.7 us -> 16.6 us
    all_to_all x4, blocking collectives: 76.2 us -> 50.2 us  [the longest x1 16.1 us: per_device(): terms = lax.all_to_all(zh_message(terms, nzh), 'zh', 0, 0, tiled=True)]
    all_to_all x2, starting transfers between devices: 8.72 us -> 21.5 us  [the longest x1 16.9 us: per_device(): first = lax.all_to_all(first, ('zh', 'zl', 'core'), 0, 0, tiled=True)]
    pallas_call x6 -> x8, Pallas kernels: 3.27 us -> 13.5 us  [small_call(): pl.pallas_call(kernel, in_specs=[SMEM if a.dtype == jnp.int32 else VMEM f...]
    pallas_call x1 -> x2, Pallas kernels: 11.4 us -> 3.03 us  [the longest x1 1.84 us: message(): pl.pallas_call(functools.partial(message_kernel, groups, nz, rows_out), i...]
    all_to_all x2, waiting for transfers between devices: 15.8 us -> 22.2 us  [the longest x1 12.8 us: per_device(): first = lax.all_to_all(first, ('zh', 'zl', 'core'), 0, 0, tiled=True)]
    ppermute x2, starting transfers between devices: 10.4 us -> 5.89 us  [the longest x1 3.75 us: per_device(): lax.ppermute(other_out, 'core', swap)]
    ppermute x2, waiting for transfers between devices: 2.95 us -> 0.6 us  [the longest x1 0.6 us: per_device(): lax.ppermute(other_out, 'core', swap)]
    unnamed x18 -> x12, local copies, waits for them, and re-layouts: 2.85 us -> 1.69 us
  transfers between devices with their start and end apart: 4 -> 4, of which waited for: 4 -> 3; matrix products, arithmetic and copies ran while one was open for 0% -> 0% of each run, Pallas kernels for 1% -> 3%
where the time goes in v3:
time: 120 us
  blocking collectives  50.2 us (42%)
  starting transfers between devices  27.4 us (23%)
  waiting for transfers between devices  22.8 us (19%)
  Pallas kernels  16.6 us (14%)
  local copies, waits for them, and re-layouts  1.74 us (1%)
    all_to_all x1, starting transfers between devices, per_device(): first = lax.all_to_all(first, ('zh', 'zl', 'core'), 0, 0, tiled=True)  16.9 us
    all_to_all x1, blocking collectives, per_device(): terms = lax.all_to_all(zh_message(terms, nzh), 'zh', 0, 0, tiled=True)  16.1 us
    pallas_call x8, Pallas kernels, small_call(): pl.pallas_call(kernel, in_specs=[SMEM if a.dtype == jnp.int32 else VMEM f...  13.5 us
    all_to_all x1, waiting for transfers between devices, per_device(): first = lax.all_to_all(first, ('zh', 'zl', 'core'), 0, 0, tiled=True)  12.8 us
    all_to_all x1, blocking collectives, per_device(): weights = lax.all_to_all(weights, ('dp', 'x'), 0, 0, tiled=True)  12 us
    all_to_all x1, blocking collectives, per_device(): beacons = lax.all_to_all(beacons, 'x', 0, 0, tiled=True)  11.4 us
    all_to_all x1, blocking collectives, per_device(): lax.all_to_all(spread(terms, nzl * CORES), ('zl', 'core'), 0, 0, tiled=True)  10.7 us
    all_to_all x1, waiting for transfers between devices, per_device(): terms = lax.all_to_all(terms, ('x', 'zl'), 0, 0, tiled=True)  9.36 us
  transfers between devices with their start and end apart: 4, of which 3 were waited for; matrix products, arithmetic and copies ran while one was open for 0% of the time, Pallas kernels for 3%

profile of v3, /device:TPU:1, one launch (start us, length us, event | category | flops | bytes accessed | tf_op | source)
XLA Modules:
  0.0 119.5 jit_solution(14710000042793104444)
XLA Ops:
  0.6 0.0 copy-start
  0.6 1.8 %message.1 = bf16[256,384]{1,0:T(8,128)(2,1)} custom-call(bf16[8,256]{1,0:T(8,128)(2,1)} %bitcast.35, bf16[8,256]{1,0:T(8,128)(2,1)} %bitcast.36, bf16[8,3584]{1,0:T(8,128)(2,1)} %bitcast.34), custom_call_target="tpu_custom_call" | custom-call | bytes 524288 | tf_op jit(solution)/shard_map/message/pallas_call | solution.py:201
  2.5 0.0 copy-start.2
  2.5 0.0 copy-start.3
  2.5 16.9 %all-to-all-start = ((bf16[32,8,384]{2,1,0:T(8,128)(2,1)}), bf16[32,8,384]{2,1,0:T(8,128)(2,1)S(1)}, u32[]{:S(2)}, u32[]{:S(2)}) async-start(bf16[32,8,384]{2,1,0:T(8,128)(2,1)} %bitcast.33), calls=%async_computation | async-start | bytes 393216 | tf_op jit(solution)/shard_map/all_to_all | solution.py:392
  19.4 0.1 pad_add_fusion.place
  19.5 0.0 copy-done
  19.5 0.0 copy-done.2
  19.5 0.0 copy-done.3
  19.5 0.0 copy-start.1
  19.5 1.0 copy-done.1
  20.5 0.6 split_heads.1
  21.2 2.1 %collective-permute-start = (bf16[128,2048]{1,0:T(8,128)(2,1)S(1)}, bf16[128,2048]{1,0:T(8,128)(2,1)S(1)}, u32[]{:S(2)}, u32[]{:S(2)}) collective-permute-start(bf16[128,2048]{1,0:T(8,128)(2,1)S(1)} %get-tuple-element.27), channel_id=1, source_target_pairs={{0,1},{1,0},{2,3},{3,2},{4,5},{5,4},{6,7},{7,6},{8,9},{9,8},{10,11... | collective-permute-start | bytes 1572872 | tf_op jit(solution)/shard_map/ppermute | solution.py:394
  23.3 0.0 copy-start.4
  23.3 0.0 copy-start.5
  23.4 0.6 copy-done.4
  24.0 0.0 copy-done.5
  24.0 1.2 mask.1.bias
  25.2 0.0 collective-permute-done.other
  25.2 12.8 %all-to-all-done = bf16[32,8,384]{2,1,0:T(8,128)(2,1)S(1)} async-done(((bf16[32,8,384]{2,1,0:T(8,128)(2,1)}), bf16[32,8,384]{2,1,0:T(8,128)(2,1)S(1)}, u32[]{:S(2)}, u32[]{:S(2)}) %all-to-all-start) | async-done | bytes 196640 | tf_op jit(solution)/shard_map/all_to_all | solution.py:392
  38.1 11.4 %all_to_all.30 = bf16[4,256,256]{2,1,0:T(8,128)(2,1)S(1)} all-to-all(bf16[4,256,256]{2,1,0:T(8,128)(2,1)S(1)} %broadcast_in_dim.23), channel_id=1, replica_groups=mesh['dp'=4,'x'=4,'zh'=4,'zl'=4,'core'=2] {'x'}, dimensions={0} | all-to-all | bytes 1048576 | tf_op jit(solution)/shard_map/all_to_all | solution.py:400
  49.5 9.5 %attention.1 = (bf16[128,1152]{1,0:T(8,128)(2,1)S(1)}, bf16[128,1152]{1,0:T(8,128)(2,1)S(1)}, bf16[1024,256]{1,0:T(8,128)(2,1)}) custom-call(f32[2,1024,128]{2,1,0:T(8,128)S(1)} %mask.1.bias, bf16[128,2048]{1,0:T(8,128)(2,1)S(1)} %get-tuple-element.29.mine, bf16[128,2048]{1,0:T(8,128)(2,1)S(1)} %collective-permute-done.other, bf16[1024,256]{1,0:T(8,128)(2,1)S(1)} %bitcast.25), custom_call_target="tpu_custom_call" | custom-call | flops 2642411520 | bytes 3735552 | tf_op jit(solution)/shard_map/attention/pallas_call | solution.py:147
  59.0 4.6 %all-to-all-start.2 = ((bf16[16,64,256]{2,1,0:T(8,128)(2,1)}), bf16[16,64,256]{2,1,0:T(8,128)(2,1)S(1)}, u32[]{:S(2)}, u32[]{:S(2)}) async-start(bf16[16,64,256]{2,1,0:T(8,128)(2,1)} %bitcast.15), calls=%async_computation.2 | async-start | bytes 1048576 | tf_op jit(solution)/shard_map/all_to_all | solution.py:406
  63.6 3.8 %collective-permute-start.1 = (bf16[128,1152]{1,0:T(8,128)(2,1)S(1)}, bf16[128,1152]{1,0:T(8,128)(2,1)S(1)}, u32[]{:S(2)}, u32[]{:S(2)}) collective-permute-start(bf16[128,1152]{1,0:T(8,128)(2,1)S(1)} %get-tuple-element.34), channel_id=1, source_target_pairs={{0,1},{1,0},{2,3},{3,2},{4,5},{5,4},{6,7},{7,6},{8,9},{9,8},{10,11... | collective-permute-start | bytes 884744 | tf_op jit(solution)/shard_map/ppermute | solution.py:407
  67.4 0.6 turn.1.hidden
  67.9 0.6 collective-permute-done.1.got
  68.5 1.4 %join_heads.1 = (bf16[128,1792]{1,0:T(8,128)(2,1)}, bf16[128,256]{1,0:T(8,128)(2,1)}, bf16[128,256]{1,0:T(8,128)(2,1)}) custom-call(s32[3]{0:T(128)S(1)} %pad_add_fusion.place, bf16[128,1152]{1,0:T(8,128)(2,1)S(1)} %get-tuple-element.33.mine, bf16[128,1152]{1,0:T(8,128)(2,1)S(1)} %collective-permute-done.1.got), custom_call_target="tpu_custom_call" | custom-call | bytes 1179660 | tf_op jit(solution)/shard_map/join_heads/pallas_call | solution.py:147
  69.9 9.4 %all-to-all-done.2.got = bf16[16,64,256]{2,1,0:T(8,128)(2,1)S(1)} async-done(((bf16[16,64,256]{2,1,0:T(8,128)(2,1)}), bf16[16,64,256]{2,1,0:T(8,128)(2,1)S(1)}, u32[]{:S(2)}, u32[]{:S(2)}) %all-to-all-start.2) | async-done | bytes 524320 | tf_op jit(solution)/shard_map/all_to_all | solution.py:406
  79.3 0.1 zh_message.1
  79.4 16.1 %all_to_all.31.got = bf16[4,80,128]{2,1,0:T(8,128)(2,1)S(1)} all-to-all(bf16[4,80,128]{2,1,0:T(8,128)(2,1)S(1)} %zh_message.1), channel_id=1, replica_groups=mesh['dp'=4,'x'=4,'zh'=4,'zl'=4,'core'=2] {'zh'}, dimensions={0} | all-to-all | bytes 163840 | tf_op jit(solution)/shard_map/all_to_all | solution.py:412
  95.4 10.7 %all_to_all.32.got = bf16[8,80,128]{2,1,0:T(8,128)(2,1)S(1)} all-to-all(bf16[8,80,128]{2,1,0:T(8,128)(2,1)S(1)} %spread.1), channel_id=1, replica_groups=mesh['dp'=4,'x'=4,'zh'=4,'zl'=4,'core'=2] {'zl','core'}, dimensions={0} | all-to-all | bytes 327680 | tf_op jit(solution)/shard_map/all_to_all | solution.py:413
  106.1 0.2 weight_terms.1
  106.3 12.0 %all_to_all.33.weights = bf16[16,8,256]{2,1,0:T(8,128)(2,1)S(1)} all-to-all(bf16[16,8,256]{2,1,0:T(8,128)(2,1)S(1)} %bitcast.28), channel_id=1, replica_groups=mesh['dp'=4,'x'=4,'zh'=4,'zl'=4,'core'=2] {'dp','x'}, dimensions={0} | all-to-all | bytes 131072 | tf_op jit(solution)/shard_map/all_to_all | solution.py:416
  118.3 1.2 finish.1
  (4 shorter events, 0.1 us)
Async XLA Ops:
  0.6 18.9 %copy-start = (bf16[1,128,1792]{2,1,0:T(8,128)(2,1)S(1)}, bf16[1,128,1792]{2,1,0:T(8,128)(2,1)}, u32[]{:S(2)}) copy-start(bf16[1,128,1792]{2,1,0:T(8,128)(2,1)} %param.9) | copy-start | bytes 1376260
  2.5 17.0 %copy-start.2 = (bf16[1,128,256]{2,1,0:T(8,128)(2,1)S(1)}, bf16[1,128,256]{2,1,0:T(8,128)(2,1)}, u32[]{:S(2)}) copy-start(bf16[1,128,256]{2,1,0:T(8,128)(2,1)} %param.10) | copy-start | bytes 196612
  2.5 17.0 %copy-start.3 = (bf16[1,128,256]{2,1,0:T(8,128)(2,1)S(1)}, bf16[1,128,256]{2,1,0:T(8,128)(2,1)}, u32[]{:S(2)}) copy-start(bf16[1,128,256]{2,1,0:T(8,128)(2,1)} %param.11) | copy-start | bytes 196612
  2.5 35.5 %all-to-all-start = ((bf16[32,8,384]{2,1,0:T(8,128)(2,1)}), bf16[32,8,384]{2,1,0:T(8,128)(2,1)S(1)}, u32[]{:S(2)}, u32[]{:S(2)}) async-start(bf16[32,8,384]{2,1,0:T(8,128)(2,1)} %bitcast.33), calls=%async_computation | async-start | bytes 393216 | tf_op jit(solution)/shard_map/all_to_all | solution.py:392
  19.5 1.0 copy-start.1
  21.2 4.0 %collective-permute-start = (bf16[128,2048]{1,0:T(8,128)(2,1)S(1)}, bf16[128,2048]{1,0:T(8,128)(2,1)S(1)}, u32[]{:S(2)}, u32[]{:S(2)}) collective-permute-start(bf16[128,2048]{1,0:T(8,128)(2,1)S(1)} %get-tuple-element.27), channel_id=1, source_target_pairs={{0,1},{1,0},{2,3},{3,2},{4,5},{5,4},{6,7},{7,6},{8,9},{9,8},{10,11... | collective-permute-start | bytes 1572872 | tf_op jit(solution)/shard_map/ppermute | solution.py:394
  23.3 0.7 copy-start.4
  23.3 0.7 copy-start.5
  59.0 20.3 %all-to-all-start.2 = ((bf16[16,64,256]{2,1,0:T(8,128)(2,1)}), bf16[16,64,256]{2,1,0:T(8,128)(2,1)S(1)}, u32[]{:S(2)}, u32[]{:S(2)}) async-start(bf16[16,64,256]{2,1,0:T(8,128)(2,1)} %bitcast.15), calls=%async_computation.2 | async-start | bytes 1048576 | tf_op jit(solution)/shard_map/all_to_all | solution.py:406
  63.6 4.9 %collective-permute-start.1 = (bf16[128,1152]{1,0:T(8,128)(2,1)S(1)}, bf16[128,1152]{1,0:T(8,128)(2,1)S(1)}, u32[]{:S(2)}, u32[]{:S(2)}) collective-permute-start(bf16[128,1152]{1,0:T(8,128)(2,1)S(1)} %get-tuple-element.34), channel_id=1, source_target_pairs={{0,1},{1,0},{2,3},{3,2},{4,5},{5,4},{6,7},{7,6},{8,9},{9,8},{10,11... | collective-permute-start | bytes 884744 | tf_op jit(solution)/shard_map/ppermute | solution.py:407

commit v4 on v3

--- a/solution.py
+++ b/solution.py
@@ -18,7 +18,7 @@
 LOG2E = math.log2(math.e)
 CORES = 2
 SUB = 8
-HEADS = 4
+HEADS = 7
 F32 = jnp.float32
 BF16 = jnp.bfloat16
 
@@ -43,8 +43,8 @@
 def attention_kernel(
     nx, nzh, nzl, slots,
     bias, mine, other, beacons,
-    own_out, other_out, terms,
-    kcat, vcat, qcat, ucat, probs, dscores,
+    terms, dscores, own_probs,
+    kcat, vcat, qcat, ucat, probs,
 ):
     span = mine.shape[0]
     wide = GROUPS * HD
@@ -85,28 +85,54 @@
             inv = 1.0 / jnp.sum(e, axis=0, keepdims=True)
             delta = jnp.sum(e * dp, axis=0, keepdims=True) * inv
             p = e * inv
-            probs[:, rows] = p.astype(BF16)
+            own_probs[:, rows] = p[0:span, :].astype(BF16)
+            probs[:, rows] = p[span:, :].astype(BF16)
             dscores[:, rows] = (p * (dp - delta)).astype(BF16)
 
-    products = ((0, dscores, qcat, SCALE), (1, probs, ucat, 1.0))
+    products = ((0, dscores[span:, :], qcat, SCALE), (1, probs[...], ucat, 1.0))
     for kind, left, right, scale in products:
-        full = jnp.dot(left[span:, :], right[...], preferred_element_type=F32) * scale
+        full = jnp.dot(left, right[...], preferred_element_type=F32) * scale
         count = full.shape[0]
         full = full.reshape(nx, nzh, nzl, CORES * slots, HD)
         full = jnp.swapaxes(full, 1, 2).reshape(count, HD)
         terms[:, kind * HD : (kind + 1) * HD] = full.astype(BF16)
-    for r, out in enumerate((own_out, other_out)):
+
+
+def own_kernel(dscores, probs, mine, other, beacons, own_out, other_out, kcat, qcat, ucat):
+    span = mine.shape[0]
+    wide = GROUPS * HD
+    kcat[span:, :] = beacons[:, 0:HD]
+    for r, (side, out) in enumerate(((mine, own_out), (other, other_out))):
+        kcat[0:span, :] = side[:, 2 * wide : 2 * wide + HD]
+        for h in range(GROUPS):
+            qcat[h * span : (h + 1) * span, :] = side[:, h * HD : (h + 1) * HD]
+            ucat[h * span : (h + 1) * span, :] = side[:, wide + h * HD : wide + (h + 1) * HD]
         rows = slice(r * wide, (r + 1) * wide)
-        for kind, left, right, scale in products:
-            part = jnp.dot(left[0:span, rows], right[rows, :], preferred_element_type=F32)
-            lo = wide + kind * HD
-            out[:, lo : lo + HD] = (part * scale).astype(BF16)
+        part = jnp.dot(dscores[0:span, rows], qcat[...], preferred_element_type=F32)
+        out[:, wide : wide + HD] = (part * SCALE).astype(BF16)
+        part = jnp.dot(probs[:, rows], ucat[...], preferred_element_type=F32)
+        out[:, wide + HD :] = part.astype(BF16)
         part = lax.dot_general(
-            kcat[r], dscores[:, rows], contract_first, preferred_element_type=F32
+            kcat[...], dscores[:, rows], (((0,), (0,)), ((), ())), preferred_element_type=F32
         ) * SCALE
         for h in range(GROUPS):
             lanes = slice(h * HD, (h + 1) * HD)
             out[:, lanes] = part[:, h * span : (h + 1) * span].T.astype(BF16)
+
+
+def own_grads(dscores, probs, mine, other, beacons):
+    span = mine.shape[0]
+    keys, columns = dscores.shape
+    shape = bf16(span, GROUPS * HD + 2 * HD)
+    return small_call(
+        own_kernel, "own_grads", [shape, shape], dscores, probs, mine, other, beacons,
+        flops=2 * keys * columns * HD,
+        scratch=[
+            pltpu.VMEM((keys, HD), BF16),
+            pltpu.VMEM((GROUPS * span, HD), BF16),
+            pltpu.VMEM((GROUPS * span, HD), BF16),
+        ],
+    )
 
 
 def attention(bias, mine, other, beacons, nx, nzh, nzl, slots):
@@ -116,16 +142,15 @@
     wide = GROUPS * HD
     return small_call(
         functools.partial(attention_kernel, nx, nzh, nzl, slots), "attention",
-        [bf16(span, wide + lanes), bf16(span, wide + lanes), bf16(total, lanes)],
+        [bf16(total, lanes), bf16(keys, CORES * wide), bf16(span, CORES * wide)],
         bias, mine, other, beacons,
-        flops=5 * 2 * QH * span * keys * HD,
+        flops=4 * 2 * QH * span * keys * HD,
         scratch=[
             pltpu.VMEM((CORES, keys, HD), BF16),
             pltpu.VMEM((CORES, keys, HD), BF16),
             pltpu.VMEM((CORES * wide, HD), BF16),
             pltpu.VMEM((CORES * wide, HD), BF16),
-            pltpu.VMEM((keys, CORES * wide), BF16),
-            pltpu.VMEM((keys, CORES * wide), BF16),
+            pltpu.VMEM((total, CORES * wide), BF16),
         ],
     )
 
@@ -346,9 +371,8 @@
     )[0]
 
 
-def finish_kernel(nzl, slots, rows, place, got, weights, keys, values, weight_grad, held):
-    zh, zl = place[1] // nzl, place[1] % nzl
-    core = place[2]
+def finish_kernel(slots, rows, got, weights, keys, values, weight_grad, held):
+    zh, zl, core = (lax.axis_index(axis) for axis in ("zh", "zl", "core"))
     key_row = pl.multiple_of((zh * CORES + core) * slots, slots)
     value_row = pl.multiple_of(rows + core * slots, slots)
     for c in range(CORES):
@@ -359,16 +383,16 @@
     weight_grad[...] = add_blocks(weights)[0 : weight_grad.shape[0], :]
 
 
-def finish(place, got, weights, nzl, slots, rows, rows_out):
+def finish(got, weights, slots, rows, rows_out):
     width = weights.shape[2]
     return small_call(
-        functools.partial(finish_kernel, nzl, slots, rows), "finish",
+        functools.partial(finish_kernel, slots, rows), "finish",
         [
             bf16(slots, width),
             bf16(slots, width),
             jax.ShapeDtypeStruct((rows_out, width), F32),
         ],
-        place, got, weights, scratch=[pltpu.VMEM((CORES, *got.shape[1:]), F32)],
+        got, weights, scratch=[pltpu.VMEM((CORES, *got.shape[1:]), F32)],
     )
 
 
@@ -400,10 +424,11 @@
     beacons = lax.all_to_all(beacons, "x", 0, 0, tiled=True)
     beacons = beacons.reshape(nx * nz * CORES * slots, width)
 
-    own_out, other_out, terms = attention(bias, mine, other, beacons, nx, nzh, nzl, slots)
+    terms, dscores, probs = attention(bias, mine, other, beacons, nx, nzh, nzl, slots)
 
     terms = terms.reshape(nx * nzl, nzh * CORES * slots, width)
     terms = lax.all_to_all(terms, ("x", "zl"), 0, 0, tiled=True)
+    own_out, other_out = own_grads(dscores, probs, mine, other, beacons)
     dq, dk, dv = join_heads(place, own_out, lax.ppermute(other_out, "core", swap))
     hidden = first[:, :, width:].reshape(nz * CORES * slots, HD)
     hidden = turn(hidden, groups, nzh, nzl, slots)
@@ -414,7 +439,7 @@
     depth = nzh * CORES * slots
     weights = weight_terms(hidden, terms, depth).reshape(groups, SUB, width)
     weights = lax.all_to_all(weights, ("dp", "x"), 0, 0, tiled=True)
-    beacon_dk, beacon_dv, weight_grad = finish(place, terms, weights, nzl, slots, depth, rows_out)
+    beacon_dk, beacon_dv, weight_grad = finish(terms, weights, slots, depth, rows_out)
     return (dq[None], dk[None], dv[None], beacon_dk[None], beacon_dv[None], weight_grad)
 
 

time: 120 us -> 119 us (level)
  waiting for transfers between devices: 22.8 us -> 15.9 us
  local copies, waits for them, and re-layouts: 1.74 us -> 5.07 us
  Pallas kernels: 16.6 us -> 18.3 us
    all_to_all x1, waiting for transfers between devices: 9.36 us -> 5.81 us  [per_device(): terms = lax.all_to_all(terms, ('x', 'zl'), 0, 0, tiled=True)]
    unnamed x12, local copies, waits for them, and re-layouts: 1.69 us -> 5.02 us
    all_to_all x1, waiting for transfers between devices: 12.8 us -> 9.51 us  [per_device(): first = lax.all_to_all(first, ('zh', 'zl', 'core'), 0, 0, tiled=True)]
    pallas_call x8 -> x9, Pallas kernels: 13.5 us -> 15.3 us  [small_call(): pl.pallas_call(kernel, in_specs=[SMEM if a.dtype == jnp.int32 else VMEM f...]
  transfers between devices with their start and end apart: 4 -> 4, of which waited for: 3 -> 3; matrix products, arithmetic and copies ran while one was open for 0% -> 0% of each run, Pallas kernels for 3% -> 6%
where the time goes in v4:
time: 119 us; the launch traced here: 118 us
  blocking collectives  50.2 us (42%)
  starting transfers between devices  27.2 us (23%)
  Pallas kernels  18.3 us (15%)
  waiting for transfers between devices  15.9 us (13%)
  local copies, waits for them, and re-layouts  5.07 us (4%)
    all_to_all x1, starting transfers between devices, per_device(): first = lax.all_to_all(first, ('zh', 'zl', 'core'), 0, 0, tiled=True)  16.8 us
    all_to_all x1, blocking collectives, per_device(): terms = lax.all_to_all(zh_message(terms, nzh), 'zh', 0, 0, tiled=True)  16.1 us
    pallas_call x9, Pallas kernels, small_call(): pl.pallas_call(kernel, in_specs=[SMEM if a.dtype == jnp.int32 else VMEM f...  15.3 us
    all_to_all x1, blocking collectives, per_device(): weights = lax.all_to_all(weights, ('dp', 'x'), 0, 0, tiled=True)  12 us
    all_to_all x1, blocking collectives, per_device(): beacons = lax.all_to_all(beacons, 'x', 0, 0, tiled=True)  11.4 us
    all_to_all x1, blocking collectives, per_device(): lax.all_to_all(spread(terms, nzl * CORES), ('zl', 'core'), 0, 0, tiled=True)  10.7 us
    all_to_all x1, waiting for transfers between devices, per_device(): first = lax.all_to_all(first, ('zh', 'zl', 'core'), 0, 0, tiled=True)  9.51 us
    all_to_all x1, waiting for transfers between devices, per_device(): terms = lax.all_to_all(terms, ('x', 'zl'), 0, 0, tiled=True)  5.81 us
  transfers between devices with their start and end apart: 4, of which 3 were waited for; matrix products, arithmetic and copies ran while one was open for 0% of the time, Pallas kernels for 6%

profile of v4, /device:TPU:1, one launch (start us, length us, event | category | flops | bytes accessed | tf_op | source)
XLA Modules:
  0.0 117.5 jit_solution(13987431093507728214)
XLA Ops:
  0.6 1.8 %message.1 = bf16[256,384]{1,0:T(8,128)(2,1)} custom-call(bf16[8,256]{1,0:T(8,128)(2,1)} %bitcast.36, bf16[8,256]{1,0:T(8,128)(2,1)} %bitcast.37, bf16[8,3584]{1,0:T(8,128)(2,1)} %bitcast.35), custom_call_target="tpu_custom_call" | custom-call | bytes 524288 | tf_op jit(solution)/shard_map/message/pallas_call | solution.py:226
  2.4 16.8 %all-to-all-start = ((bf16[32,8,384]{2,1,0:T(8,128)(2,1)}), bf16[32,8,384]{2,1,0:T(8,128)(2,1)S(1)}, u32[]{:S(2)}, u32[]{:S(2)}) async-start(bf16[32,8,384]{2,1,0:T(8,128)(2,1)} %bitcast.34), calls=%async_computation | async-start | bytes 393216 | tf_op jit(solution)/shard_map/all_to_all | solution.py:416
  19.2 0.1 pad_add_fusion.place
  19.3 0.0 copy-start
  19.3 1.0 copy-done
  20.3 0.0 copy-start.1
  20.3 1.0 copy-done.1
  21.3 0.0 copy-start.2
  21.3 0.8 copy-done.2
  22.2 0.0 copy-start.3
  22.2 0.8 copy-done.3
  23.0 0.6 split_heads.1
  23.6 2.1 %collective-permute-start = (bf16[128,2048]{1,0:T(8,128)(2,1)S(1)}, bf16[128,2048]{1,0:T(8,128)(2,1)S(1)}, u32[]{:S(2)}, u32[]{:S(2)}) collective-permute-start(bf16[128,2048]{1,0:T(8,128)(2,1)S(1)} %get-tuple-element.29), channel_id=1, source_target_pairs={{0,1},{1,0},{2,3},{3,2},{4,5},{5,4},{6,7},{7,6},{8,9},{9,8},{10,11... | collective-permute-start | bytes 1572872 | tf_op jit(solution)/shard_map/ppermute | solution.py:418
  25.8 0.0 copy-start.4
  25.8 0.6 copy-done.4
  26.5 0.0 copy-start.5
  26.5 0.7 copy-done.5
  27.1 1.2 %mask.1.bias = f32[2,1024,128]{2,1,0:T(8,128)S(1)} custom-call(s32[3]{0:T(128)S(1)} %pad_add_fusion.place, s32[128]{0:T(128)S(1)} %copy-done.4, s32[1,128]{1,0:T(1,128)S(1)} %bitcast.32, s32[1,128]{1,0:T(1,128)S(1)} %bitcast.33), custom_call_target="tpu_custom_call" | custom-call | bytes 2097152 | tf_op jit(solution)/shard_map/mask/pallas_call | solution.py:288
  28.3 0.0 collective-permute-done.other
  28.3 9.5 %all-to-all-done = bf16[32,8,384]{2,1,0:T(8,128)(2,1)S(1)} async-done(((bf16[32,8,384]{2,1,0:T(8,128)(2,1)}), bf16[32,8,384]{2,1,0:T(8,128)(2,1)S(1)}, u32[]{:S(2)}, u32[]{:S(2)}) %all-to-all-start) | async-done | bytes 196640 | tf_op jit(solution)/shard_map/all_to_all | solution.py:416
  37.9 11.4 %all_to_all.30 = bf16[4,256,256]{2,1,0:T(8,128)(2,1)S(1)} all-to-all(bf16[4,256,256]{2,1,0:T(8,128)(2,1)S(1)} %broadcast_in_dim.23), channel_id=1, replica_groups=mesh['dp'=4,'x'=4,'zh'=4,'zl'=4,'core'=2] {'x'}, dimensions={0} | all-to-all | bytes 1048576 | tf_op jit(solution)/shard_map/all_to_all | solution.py:424
  49.3 8.3 %attention.1 = (bf16[1024,256]{1,0:T(8,128)(2,1)}, bf16[1152,1792]{1,0:T(8,128)(2,1)}, bf16[128,1792]{1,0:T(8,128)(2,1)S(1)}) custom-call(f32[2,1024,128]{2,1,0:T(8,128)S(1)} %mask.1.bias, bf16[128,2048]{1,0:T(8,128)(2,1)S(1)} %get-tuple-element.31.mine, bf16[128,2048]{1,0:T(8,128)(2,1)S(1)} %collective-permute-done.other, bf16[1024,256]{1,0:T(8,128)(2,1)S(1)} %bitcast.25), custom_call_target="tpu_custom_call" | custom-call | flops 2113929216 | bytes 7733248 | tf_op jit(solution)/shard_map/attention/pallas_call | solution.py:172
  57.6 4.6 %all-to-all-start.2 = ((bf16[16,64,256]{2,1,0:T(8,128)(2,1)}), bf16[16,64,256]{2,1,0:T(8,128)(2,1)S(1)}, u32[]{:S(2)}, u32[]{:S(2)}) async-start(bf16[16,64,256]{2,1,0:T(8,128)(2,1)} %bitcast.15), calls=%async_computation.2 | async-start | bytes 1048576 | tf_op jit(solution)/shard_map/all_to_all | solution.py:430
  62.1 3.5 %own_grads.1 = (bf16[128,1152]{1,0:T(8,128)(2,1)S(1)}, bf16[128,1152]{1,0:T(8,128)(2,1)S(1)}) custom-call(bf16[1152,1792]{1,0:T(8,128)(2,1)} %get-tuple-element.35.dscores, bf16[128,1792]{1,0:T(8,128)(2,1)S(1)} %get-tuple-element.36.probs, bf16[128,2048]{1,0:T(8,128)(2,1)S(1)} %get-tuple-element.31.mine, bf16[128,2048]{1,0:T(8,128)(2,1)S(1)} %collective-permute-done.other, ...), custom_call_target="tpu_custom_call" | custom-call | flops 528482304 | bytes 6750208 | tf_op jit(solution)/shard_map/own_grads/pallas_call | solution.py:172
  65.7 3.8 %collective-permute-start.1 = (bf16[128,1152]{1,0:T(8,128)(2,1)S(1)}, bf16[128,1152]{1,0:T(8,128)(2,1)S(1)}, u32[]{:S(2)}, u32[]{:S(2)}) collective-permute-start(bf16[128,1152]{1,0:T(8,128)(2,1)S(1)} %get-tuple-element.38), channel_id=1, source_target_pairs={{0,1},{1,0},{2,3},{3,2},{4,5},{5,4},{6,7},{7,6},{8,9},{9,8},{10,11... | collective-permute-start | bytes 884744 | tf_op jit(solution)/shard_map/ppermute | solution.py:432
  69.5 0.6 turn.1.hidden
  70.0 0.6 collective-permute-done.1.got
  70.6 1.4 %join_heads.1 = (bf16[128,1792]{1,0:T(8,128)(2,1)}, bf16[128,256]{1,0:T(8,128)(2,1)}, bf16[128,256]{1,0:T(8,128)(2,1)}) custom-call(s32[3]{0:T(128)S(1)} %pad_add_fusion.place, bf16[128,1152]{1,0:T(8,128)(2,1)S(1)} %get-tuple-element.37.mine, bf16[128,1152]{1,0:T(8,128)(2,1)S(1)} %collective-permute-done.1.got), custom_call_target="tpu_custom_call" | custom-call | bytes 1179660 | tf_op jit(solution)/shard_map/join_heads/pallas_call | solution.py:172
  72.0 5.8 %all-to-all-done.2.got = bf16[16,64,256]{2,1,0:T(8,128)(2,1)S(1)} async-done(((bf16[16,64,256]{2,1,0:T(8,128)(2,1)}), bf16[16,64,256]{2,1,0:T(8,128)(2,1)S(1)}, u32[]{:S(2)}, u32[]{:S(2)}) %all-to-all-start.2) | async-done | bytes 524320 | tf_op jit(solution)/shard_map/all_to_all | solution.py:430
  77.8 0.1 zh_message.1
  77.9 16.1 %all_to_all.31.got = bf16[4,80,128]{2,1,0:T(8,128)(2,1)S(1)} all-to-all(bf16[4,80,128]{2,1,0:T(8,128)(2,1)S(1)} %zh_message.1), channel_id=1, replica_groups=mesh['dp'=4,'x'=4,'zh'=4,'zl'=4,'core'=2] {'zh'}, dimensions={0} | all-to-all | bytes 163840 | tf_op jit(solution)/shard_map/all_to_all | solution.py:437
  94.0 10.7 %all_to_all.32.got = bf16[8,80,128]{2,1,0:T(8,128)(2,1)S(1)} all-to-all(bf16[8,80,128]{2,1,0:T(8,128)(2,1)S(1)} %spread.1), channel_id=1, replica_groups=mesh['dp'=4,'x'=4,'zh'=4,'zl'=4,'core'=2] {'zl','core'}, dimensions={0} | all-to-all | bytes 327680 | tf_op jit(solution)/shard_map/all_to_all | solution.py:438
  104.7 0.2 weight_terms.1
  104.9 12.0 %all_to_all.33.weights = bf16[16,8,256]{2,1,0:T(8,128)(2,1)S(1)} all-to-all(bf16[16,8,256]{2,1,0:T(8,128)(2,1)S(1)} %bitcast.29), channel_id=1, replica_groups=mesh['dp'=4,'x'=4,'zh'=4,'zl'=4,'core'=2] {'dp','x'}, dimensions={0} | all-to-all | bytes 131072 | tf_op jit(solution)/shard_map/all_to_all | solution.py:441
  116.9 0.6 finish.1
  (4 shorter events, 0.1 us)
Async XLA Ops:
  2.4 35.4 %all-to-all-start = ((bf16[32,8,384]{2,1,0:T(8,128)(2,1)}), bf16[32,8,384]{2,1,0:T(8,128)(2,1)S(1)}, u32[]{:S(2)}, u32[]{:S(2)}) async-start(bf16[32,8,384]{2,1,0:T(8,128)(2,1)} %bitcast.34), calls=%async_computation | async-start | bytes 393216 | tf_op jit(solution)/shard_map/all_to_all | solution.py:416
  19.3 1.0 copy-start
  20.3 1.0 copy-start.1
  21.3 0.8 copy-start.2
  22.2 0.8 copy-start.3
  23.6 4.7 %collective-permute-start = (bf16[128,2048]{1,0:T(8,128)(2,1)S(1)}, bf16[128,2048]{1,0:T(8,128)(2,1)S(1)}, u32[]{:S(2)}, u32[]{:S(2)}) collective-permute-start(bf16[128,2048]{1,0:T(8,128)(2,1)S(1)} %get-tuple-element.29), channel_id=1, source_target_pairs={{0,1},{1,0},{2,3},{3,2},{4,5},{5,4},{6,7},{7,6},{8,9},{9,8},{10,11... | collective-permute-start | bytes 1572872 | tf_op jit(solution)/shard_map/ppermute | solution.py:418
  25.8 0.7 copy-start.4
  26.5 0.7 copy-start.5
  57.6 20.3 %all-to-all-start.2 = ((bf16[16,64,256]{2,1,0:T(8,128)(2,1)}), bf16[16,64,256]{2,1,0:T(8,128)(2,1)S(1)}, u32[]{:S(2)}, u32[]{:S(2)}) async-start(bf16[16,64,256]{2,1,0:T(8,128)(2,1)} %bitcast.15), calls=%async_computation.2 | async-start | bytes 1048576 | tf_op jit(solution)/shard_map/all_to_all | solution.py:430
  65.7 5.0 %collective-permute-start.1 = (bf16[128,1152]{1,0:T(8,128)(2,1)S(1)}, bf16[128,1152]{1,0:T(8,128)(2,1)S(1)}, u32[]{:S(2)}, u32[]{:S(2)}) collective-permute-start(bf16[128,1152]{1,0:T(8,128)(2,1)S(1)} %get-tuple-element.38), channel_id=1, source_target_pairs={{0,1},{1,0},{2,3},{3,2},{4,5},{5,4},{6,7},{7,6},{8,9},{9,8},{10,11... | collective-permute-start | bytes 884744 | tf_op jit(solution)/shard_map/ppermute | solution.py:432

commit v5 on v4

--- a/solution.py
+++ b/solution.py
@@ -101,38 +101,58 @@
 def own_kernel(dscores, probs, mine, other, beacons, own_out, other_out, kcat, qcat, ucat):
     span = mine.shape[0]
     wide = GROUPS * HD
-    kcat[span:, :] = beacons[:, 0:HD]
-    for r, (side, out) in enumerate(((mine, own_out), (other, other_out))):
+
+    def rows_of(side, out):
         kcat[0:span, :] = side[:, 2 * wide : 2 * wide + HD]
+        kcat[span:, :] = beacons[...]
         for h in range(GROUPS):
             qcat[h * span : (h + 1) * span, :] = side[:, h * HD : (h + 1) * HD]
             ucat[h * span : (h + 1) * span, :] = side[:, wide + h * HD : wide + (h + 1) * HD]
-        rows = slice(r * wide, (r + 1) * wide)
-        part = jnp.dot(dscores[0:span, rows], qcat[...], preferred_element_type=F32)
+        part = jnp.dot(dscores[0:span, :], qcat[...], preferred_element_type=F32)
         out[:, wide : wide + HD] = (part * SCALE).astype(BF16)
-        part = jnp.dot(probs[:, rows], ucat[...], preferred_element_type=F32)
+        part = jnp.dot(probs[...], ucat[...], preferred_element_type=F32)
         out[:, wide + HD :] = part.astype(BF16)
         part = lax.dot_general(
-            kcat[...], dscores[:, rows], (((0,), (0,)), ((), ())), preferred_element_type=F32
+            kcat[...], dscores[...], (((0,), (0,)), ((), ())), preferred_element_type=F32
         ) * SCALE
         for h in range(GROUPS):
             lanes = slice(h * HD, (h + 1) * HD)
             out[:, lanes] = part[:, h * span : (h + 1) * span].T.astype(BF16)
 
+    pl.when(pl.program_id(0) == 0)(lambda: rows_of(mine, own_out))
+    pl.when(pl.program_id(0) == 1)(lambda: rows_of(other, other_out))
+
 
 def own_grads(dscores, probs, mine, other, beacons):
     span = mine.shape[0]
     keys, columns = dscores.shape
-    shape = bf16(span, GROUPS * HD + 2 * HD)
-    return small_call(
-        own_kernel, "own_grads", [shape, shape], dscores, probs, mine, other, beacons,
-        flops=2 * keys * columns * HD,
-        scratch=[
+    wide = GROUPS * HD
+    shape = bf16(span, wide + 2 * HD)
+    whole = pl.BlockSpec(mine.shape, lambda r: (0, 0))
+    result = pl.BlockSpec(shape.shape, lambda r: (0, 0))
+    return pl.pallas_call(
+        own_kernel,
+        grid=(CORES,),
+        in_specs=[
+            pl.BlockSpec((keys, wide), lambda r: (0, r)),
+            pl.BlockSpec((span, wide), lambda r: (0, r)),
+            whole,
+            whole,
+            pl.BlockSpec((beacons.shape[0], HD), lambda r: (0, 0)),
+        ],
+        out_specs=[result, result],
+        out_shape=[shape, shape],
+        scratch_shapes=[
             pltpu.VMEM((keys, HD), BF16),
-            pltpu.VMEM((GROUPS * span, HD), BF16),
-            pltpu.VMEM((GROUPS * span, HD), BF16),
+            pltpu.VMEM((wide, HD), BF16),
+            pltpu.VMEM((wide, HD), BF16),
         ],
-    )
+        compiler_params=pltpu.CompilerParams(vmem_limit_bytes=48 * 1024 * 1024),
+        cost_estimate=pl.CostEstimate(
+            flops=2 * keys * columns * HD, bytes_accessed=6 * 1024 * 1024, transcendentals=0
+        ),
+        name="own_grads",
+    )(dscores, probs, mine, other, beacons)
 
 
 def attention(bias, mine, other, beacons, nx, nzh, nzl, slots):
@@ -240,9 +260,9 @@
     )(keys, values, hidden)
 
 
-def split_kernel(place, q, up, k, v, mine, send):
-    wide = GROUPS * HD
-    core = place[2]
+def split_kernel(q, up, k, v, mine, send):
+    wide = GROUPS * HD
+    core = lax.axis_index("core")
     for out, head in ((mine, core), (send, 1 - core)):
         lanes = pl.ds(pl.multiple_of(head * wide, HD), wide)
         out[:, 0:wide] = q[:, lanes]
@@ -252,14 +272,14 @@
         out[:, 2 * wide + HD :] = v[:, lanes]
 
 
-def split_heads(place, q, up, k, v):
+def split_heads(q, up, k, v):
     shape = bf16(q.shape[0], 2 * GROUPS * HD + 2 * HD)
-    return small_call(split_kernel, "split_heads", [shape, shape], place, q, up, k, v)
-
-
-def join_kernel(place, mine, got, dq, dk, dv):
-    wide = GROUPS * HD
-    core = place[2]
+    return small_call(split_kernel, "split_heads", [shape, shape], q, up, k, v)
+
+
+def join_kernel(mine, got, dq, dk, dv):
+    wide = GROUPS * HD
+    core = lax.axis_index("core")
     for part, head in ((mine, core), (got, 1 - core)):
         dq[:, pl.ds(pl.multiple_of(head * wide, HD), wide)] = part[:, 0:wide]
         lanes = pl.ds(pl.multiple_of(head * HD, HD), HD)
@@ -267,15 +287,15 @@
         dv[:, lanes] = part[:, wide + HD :]
 
 
-def join_heads(place, mine, got):
+def join_heads(mine, got):
     span = mine.shape[0]
     shapes = [bf16(span, QH * HD), bf16(span, KVH * HD), bf16(span, KVH * HD)]
-    return small_call(join_kernel, "join_heads", shapes, place, mine, got)
-
-
-def mask_kernel(nz, slots, span, place, order_s, order_row, ratio_row, bias):
-    core = place[2]
-    first = (place[0] * nz + place[1]) * CORES
+    return small_call(join_kernel, "join_heads", shapes, mine, got)
+
+
+def mask_kernel(nz, nzl, slots, span, order_s, order_row, ratio_row, bias):
+    x, zh, zl, core = (lax.axis_index(axis) for axis in ("x", "zh", "zl", "core"))
+    first = (x * nz + zh * nzl + zl) * CORES
     for r, index in enumerate((first + core, first + 1 - core)):
         owners = visible_bias(order_row[...], ratio_row[...], order_s[index], slots, span)
         for j in range(owners.shape[1]):
@@ -283,11 +303,11 @@
             bias[r, j * slots : (j + 1) * slots, :] = tile
 
 
-def mask(place, order, ratio, nz, slots, span):
+def mask(order, ratio, nz, nzl, slots, span):
     nseq = order.shape[0]
     return pl.pallas_call(
-        functools.partial(mask_kernel, nz, slots, span),
-        in_specs=[SMEM, SMEM, VMEM, VMEM],
+        functools.partial(mask_kernel, nz, nzl, slots, span),
+        in_specs=[SMEM, VMEM, VMEM],
         out_specs=VMEM,
         out_shape=jax.ShapeDtypeStruct((CORES, nseq * slots, HD), F32),
         compiler_params=pltpu.CompilerParams(vmem_limit_bytes=32 * 1024 * 1024),
@@ -295,7 +315,7 @@
             flops=0, bytes_accessed=2 * 1024 * 1024, transcendentals=0
         ),
         name="mask",
-    )(place, order, order.reshape(1, nseq), ratio.reshape(1, nseq))
+    )(order, order.reshape(1, nseq), ratio.reshape(1, nseq))
 
 
 def turn_kernel(groups, nzh, nzl, slots, got, out):
@@ -396,6 +416,19 @@
     )
 
 
+def near_groups(nx, nzh, nzl):
+    groups = []
+    for core in range(CORES):
+        for zh in range(nzh):
+            members = []
+            for x in range(nx):
+                for zl in range(nzl):
+                    place = zh if core == 0 or zl >= nzl // 2 else (zh + 1) % nzh
+                    members.append(((x * nzh + place) * nzl + zl) * CORES + core)
+            groups.append(members)
+    return groups
+
+
 def per_device(
     nx, nzh, nzl,
     queries, keys, values, grad_out, beacon_keys, beacon_values, beacon_hidden, order, ratio,
@@ -408,15 +441,13 @@
     groups = ndp * nx
     rows_out = model // (groups * nz * CORES)
     swap = [(0, 1), (1, 0)]
-    z_index = lax.axis_index("zh") * nzl + lax.axis_index("zl")
-    place = jnp.stack([lax.axis_index("x"), z_index, lax.axis_index("core")]).astype(jnp.int32)
 
     first = message(beacon_keys[0], beacon_values[0], beacon_hidden[0], groups, nz, rows_out)
     first = first.reshape(nz * CORES, slots, width + HD)
     first = lax.all_to_all(first, ("zh", "zl", "core"), 0, 0, tiled=True)
-    mine, send = split_heads(place, queries[0], grad_out[0], keys[0], values[0])
+    mine, send = split_heads(queries[0], grad_out[0], keys[0], values[0])
     other = lax.ppermute(send, "core", swap)
-    bias = mask(place, order, ratio, nz, slots, span)
+    bias = mask(order, ratio, nz, nzl, slots, span)
     first, mine, other, bias = lax.optimization_barrier((first, mine, other, bias))
 
     beacons = first[:, :, :width].reshape(1, nz * CORES * slots, width)
@@ -427,9 +458,12 @@
     terms, dscores, probs = attention(bias, mine, other, beacons, nx, nzh, nzl, slots)
 
     terms = terms.reshape(nx * nzl, nzh * CORES * slots, width)
-    terms = lax.all_to_all(terms, ("x", "zl"), 0, 0, tiled=True)
+    terms = lax.all_to_all(
+        terms, ("x", "zh", "zl", "core"), 0, 0, tiled=True,
+        axis_index_groups=near_groups(nx, nzh, nzl),
+    )
     own_out, other_out = own_grads(dscores, probs, mine, other, beacons)
-    dq, dk, dv = join_heads(place, own_out, lax.ppermute(other_out, "core", swap))
+    dq, dk, dv = join_heads(own_out, lax.ppermute(other_out, "core", swap))
     hidden = first[:, :, width:].reshape(nz * CORES * slots, HD)
     hidden = turn(hidden, groups, nzh, nzl, slots)
     terms, hidden, dq, dk, dv = lax.optimization_barrier((terms, hidden, dq, dk, dv))

time: 119 us -> 117 us (0.983)
  Pallas kernels: 18.3 us -> 16.9 us
    pallas_call x9 -> x8, Pallas kernels: 15.3 us -> 10.7 us  [small_call(): pl.pallas_call(kernel, in_specs=[SMEM if a.dtype == jnp.int32 else VMEM f...]
    pallas_call x1 -> x2, Pallas kernels: 1.19 us -> 4.42 us  [the longest x1 3.24 us: own_grads(): pl.pallas_call(own_kernel, grid=(CORES,), in_specs=[pl.BlockSpec((keys, w...]
  transfers between devices with their start and end apart: 4 -> 4, of which waited for: 3 -> 3; matrix products, arithmetic and copies ran while one was open for 0% -> 0% of each run, Pallas kernels for 6% -> 5%
where the time goes in v5:
time: 117 us; the launch traced here: 116 us
  blocking collectives  49.9 us (43%)
  starting transfers between devices  27.2 us (23%)
  Pallas kernels  16.9 us (14%)
  waiting for transfers between devices  16.3 us (14%)
  local copies, waits for them, and re-layouts  5.07 us (4%)
    all_to_all x1, blocking collectives, per_device(): terms = lax.all_to_all(zh_message(terms, nzh), 'zh', 0, 0, tiled=True)  17 us
    all_to_all x1, starting transfers between devices, per_device(): first = lax.all_to_all(first, ('zh', 'zl', 'core'), 0, 0, tiled=True)  16.8 us
    all_to_all x1, blocking collectives, per_device(): beacons = lax.all_to_all(beacons, 'x', 0, 0, tiled=True)  11.4 us
    all_to_all x1, blocking collectives, per_device(): weights = lax.all_to_all(weights, ('dp', 'x'), 0, 0, tiled=True)  11.3 us
    pallas_call x8, Pallas kernels, small_call(): pl.pallas_call(kernel, in_specs=[SMEM if a.dtype == jnp.int32 else VMEM f...  10.7 us
    all_to_all x1, blocking collectives, per_device(): lax.all_to_all(spread(terms, nzl * CORES), ('zl', 'core'), 0, 0, tiled=True)  10.2 us
    all_to_all x1, waiting for transfers between devices, per_device(): first = lax.all_to_all(first, ('zh', 'zl', 'core'), 0, 0, tiled=True)  10.1 us
    all_to_all x1, waiting for transfers between devices, per_device(): lax.all_to_all(terms, ('x', 'zh', 'zl', 'core'), 0, 0, tiled=True, axis_i...  5.56 us
  transfers between devices with their start and end apart: 4, of which 3 were waited for; matrix products, arithmetic and copies ran while one was open for 0% of the time, Pallas kernels for 5%

profile of v5, /device:TPU:1, one launch (start us, length us, event | category | flops | bytes accessed | tf_op | source)
XLA Modules:
  0.0 116.2 jit_solution(3301891687840124927)
XLA Ops:
  0.6 1.8 %message.1 = bf16[256,384]{1,0:T(8,128)(2,1)} custom-call(bf16[8,256]{1,0:T(8,128)(2,1)} %bitcast.33, bf16[8,256]{1,0:T(8,128)(2,1)} %bitcast.34, bf16[8,3584]{1,0:T(8,128)(2,1)} %bitcast.32), custom_call_target="tpu_custom_call" | custom-call | bytes 524288 | tf_op jit(solution)/shard_map/message/pallas_call | solution.py:246
  2.4 16.8 %all-to-all-start = ((bf16[32,8,384]{2,1,0:T(8,128)(2,1)}), bf16[32,8,384]{2,1,0:T(8,128)(2,1)S(1)}, u32[]{:S(2)}, u32[]{:S(2)}) async-start(bf16[32,8,384]{2,1,0:T(8,128)(2,1)} %bitcast.31), calls=%async_computation | async-start | bytes 393216 | tf_op jit(solution)/shard_map/all_to_all | solution.py:447
  19.2 0.0 copy-start
  19.2 1.0 copy-done
  20.2 0.0 copy-start.1
  20.2 1.0 copy-done.1
  21.2 0.0 copy-start.2
  21.2 0.8 copy-done.2
  22.1 0.0 copy-start.3
  22.1 0.8 copy-done.3
  22.9 0.1 split_heads.1
  23.0 2.1 %collective-permute-start = (bf16[128,2048]{1,0:T(8,128)(2,1)S(1)}, bf16[128,2048]{1,0:T(8,128)(2,1)S(1)}, u32[]{:S(2)}, u32[]{:S(2)}) collective-permute-start(bf16[128,2048]{1,0:T(8,128)(2,1)S(1)} %get-tuple-element.29), channel_id=1, source_target_pairs={{0,1},{1,0},{2,3},{3,2},{4,5},{5,4},{6,7},{7,6},{8,9},{9,8},{10,11... | collective-permute-start | bytes 1572872 | tf_op jit(solution)/shard_map/ppermute | solution.py:449
  25.2 0.0 copy-start.4
  25.2 0.6 copy-done.4
  25.8 0.0 copy-start.5
  25.8 0.7 copy-done.5
  26.5 1.2 %mask.1.bias = f32[2,1024,128]{2,1,0:T(8,128)S(1)} custom-call(s32[128]{0:T(128)S(1)} %copy-done.4, s32[1,128]{1,0:T(1,128)S(1)} %bitcast.29, s32[1,128]{1,0:T(1,128)S(1)} %bitcast.30), custom_call_target="tpu_custom_call" | custom-call | bytes 2097152 | tf_op jit(solution)/shard_map/mask/pallas_call | solution.py:308
  27.7 0.0 collective-permute-done.other
  27.7 10.1 %all-to-all-done = bf16[32,8,384]{2,1,0:T(8,128)(2,1)S(1)} async-done(((bf16[32,8,384]{2,1,0:T(8,128)(2,1)}), bf16[32,8,384]{2,1,0:T(8,128)(2,1)S(1)}, u32[]{:S(2)}, u32[]{:S(2)}) %all-to-all-start) | async-done | bytes 196640 | tf_op jit(solution)/shard_map/all_to_all | solution.py:447
  37.9 11.4 %all_to_all.30 = bf16[4,256,256]{2,1,0:T(8,128)(2,1)S(1)} all-to-all(bf16[4,256,256]{2,1,0:T(8,128)(2,1)S(1)} %broadcast_in_dim.23), channel_id=1, replica_groups=mesh['dp'=4,'x'=4,'zh'=4,'zl'=4,'core'=2] {'x'}, dimensions={0} | all-to-all | bytes 1048576 | tf_op jit(solution)/shard_map/all_to_all | solution.py:455
  49.3 8.3 %attention.1 = (bf16[1024,256]{1,0:T(8,128)(2,1)}, bf16[1152,1792]{1,0:T(8,128)(2,1)}, bf16[128,1792]{1,0:T(8,128)(2,1)S(1)}) custom-call(f32[2,1024,128]{2,1,0:T(8,128)S(1)} %mask.1.bias, bf16[128,2048]{1,0:T(8,128)(2,1)S(1)} %get-tuple-element.31.mine, bf16[128,2048]{1,0:T(8,128)(2,1)S(1)} %collective-permute-done.other, bf16[1024,256]{1,0:T(8,128)(2,1)S(1)} %bitcast.22), custom_call_target="tpu_custom_call" | custom-call | flops 2113929216 | bytes 7733248 | tf_op jit(solution)/shard_map/attention/pallas_call | solution.py:192
  57.6 4.0 %all-to-all-start.2 = ((bf16[16,64,256]{2,1,0:T(8,128)(2,1)}), bf16[16,64,256]{2,1,0:T(8,128)(2,1)S(1)}, u32[]{:S(2)}, u32[]{:S(2)}) async-start(bf16[16,64,256]{2,1,0:T(8,128)(2,1)} %bitcast.12), calls=%async_computation.2 | async-start | bytes 1048576 | tf_op jit(solution)/shard_map/all_to_all | solution.py:461
  61.5 3.2 %own_grads.1 = (bf16[128,1152]{1,0:T(8,128)(2,1)S(1)}, bf16[128,1152]{1,0:T(8,128)(2,1)S(1)}) custom-call(bf16[1152,1792]{1,0:T(8,128)(2,1)} %get-tuple-element.35.dscores, bf16[128,1792]{1,0:T(8,128)(2,1)S(1)} %get-tuple-element.36.probs, bf16[128,2048]{1,0:T(8,128)(2,1)S(1)} %get-tuple-element.31.mine, bf16[128,2048]{1,0:T(8,128)(2,1)S(1)} %collective-permute-done.other, ...), custom_call_target="tpu_custom_call" | custom-call | flops 528482304 | bytes 6291456 | tf_op jit(solution)/shard_map/own_grads/pallas_call | solution.py:133
  64.8 4.4 %collective-permute-start.1 = (bf16[128,1152]{1,0:T(8,128)(2,1)S(1)}, bf16[128,1152]{1,0:T(8,128)(2,1)S(1)}, u32[]{:S(2)}, u32[]{:S(2)}) collective-permute-start(bf16[128,1152]{1,0:T(8,128)(2,1)S(1)} %get-tuple-element.38), channel_id=1, source_target_pairs={{0,1},{1,0},{2,3},{3,2},{4,5},{5,4},{6,7},{7,6},{8,9},{9,8},{10,11... | collective-permute-start | bytes 884744 | tf_op jit(solution)/shard_map/ppermute | solution.py:466
  69.2 0.6 turn.1.hidden
  69.7 0.6 collective-permute-done.1.got
  70.3 0.9 join_heads.1
  71.2 5.6 %all-to-all-done.2.got = bf16[16,64,256]{2,1,0:T(8,128)(2,1)S(1)} async-done(((bf16[16,64,256]{2,1,0:T(8,128)(2,1)}), bf16[16,64,256]{2,1,0:T(8,128)(2,1)S(1)}, u32[]{:S(2)}, u32[]{:S(2)}) %all-to-all-start.2) | async-done | bytes 524320 | tf_op jit(solution)/shard_map/all_to_all | solution.py:461
  76.8 0.1 zh_message.1
  76.8 17.0 %all_to_all.31.got = bf16[4,80,128]{2,1,0:T(8,128)(2,1)S(1)} all-to-all(bf16[4,80,128]{2,1,0:T(8,128)(2,1)S(1)} %zh_message.1), channel_id=1, replica_groups=mesh['dp'=4,'x'=4,'zh'=4,'zl'=4,'core'=2] {'zh'}, dimensions={0} | all-to-all | bytes 163840 | tf_op jit(solution)/shard_map/all_to_all | solution.py:471
  93.9 10.2 %all_to_all.32.got = bf16[8,80,128]{2,1,0:T(8,128)(2,1)S(1)} all-to-all(bf16[8,80,128]{2,1,0:T(8,128)(2,1)S(1)} %spread.1), channel_id=1, replica_groups=mesh['dp'=4,'x'=4,'zh'=4,'zl'=4,'core'=2] {'zl','core'}, dimensions={0} | all-to-all | bytes 327680 | tf_op jit(solution)/shard_map/all_to_all | solution.py:472
  104.1 0.2 weight_terms.1
  104.3 11.3 %all_to_all.33.weights = bf16[16,8,256]{2,1,0:T(8,128)(2,1)S(1)} all-to-all(bf16[16,8,256]{2,1,0:T(8,128)(2,1)S(1)} %bitcast.26), channel_id=1, replica_groups=mesh['dp'=4,'x'=4,'zh'=4,'zl'=4,'core'=2] {'dp','x'}, dimensions={0} | all-to-all | bytes 131072 | tf_op jit(solution)/shard_map/all_to_all | solution.py:475
  115.6 0.6 finish.1
  (4 shorter events, 0.1 us)
Async XLA Ops:
  2.4 35.4 %all-to-all-start = ((bf16[32,8,384]{2,1,0:T(8,128)(2,1)}), bf16[32,8,384]{2,1,0:T(8,128)(2,1)S(1)}, u32[]{:S(2)}, u32[]{:S(2)}) async-start(bf16[32,8,384]{2,1,0:T(8,128)(2,1)} %bitcast.31), calls=%async_computation | async-start | bytes 393216 | tf_op jit(solution)/shard_map/all_to_all | solution.py:447
  19.2 1.0 copy-start
  20.2 1.0 copy-start.1
  21.2 0.8 copy-start.2
  22.1 0.8 copy-start.3
  23.0 4.7 %collective-permute-start = (bf16[128,2048]{1,0:T(8,128)(2,1)S(1)}, bf16[128,2048]{1,0:T(8,128)(2,1)S(1)}, u32[]{:S(2)}, u32[]{:S(2)}) collective-permute-start(bf16[128,2048]{1,0:T(8,128)(2,1)S(1)} %get-tuple-element.29), channel_id=1, source_target_pairs={{0,1},{1,0},{2,3},{3,2},{4,5},{5,4},{6,7},{7,6},{8,9},{9,8},{10,11... | collective-permute-start | bytes 1572872 | tf_op jit(solution)/shard_map/ppermute | solution.py:449
  25.2 0.7 copy-start.4
  25.8 0.7 copy-start.5
  57.6 19.2 %all-to-all-start.2 = ((bf16[16,64,256]{2,1,0:T(8,128)(2,1)}), bf16[16,64,256]{2,1,0:T(8,128)(2,1)S(1)}, u32[]{:S(2)}, u32[]{:S(2)}) async-start(bf16[16,64,256]{2,1,0:T(8,128)(2,1)} %bitcast.12), calls=%async_computation.2 | async-start | bytes 1048576 | tf_op jit(solution)/shard_map/all_to_all | solution.py:461
  64.8 5.5 %collective-permute-start.1 = (bf16[128,1152]{1,0:T(8,128)(2,1)S(1)}, bf16[128,1152]{1,0:T(8,128)(2,1)S(1)}, u32[]{:S(2)}, u32[]{:S(2)}) collective-permute-start(bf16[128,1152]{1,0:T(8,128)(2,1)S(1)} %get-tuple-element.38), channel_id=1, source_target_pairs={{0,1},{1,0},{2,3},{3,2},{4,5},{5,4},{6,7},{7,6},{8,9},{9,8},{10,11... | collective-permute-start | bytes 884744 | tf_op jit(solution)/shard_map/ppermute | solution.py:466

commit v6 on v5

--- a/solution.py
+++ b/solution.py
@@ -327,12 +327,13 @@
     from_lane = lax.broadcasted_iota(jnp.int32, (HD, width), 0)
     to_lane = lax.broadcasted_iota(jnp.int32, (HD, width), 1)
     total = jnp.zeros((count, width), F32)
+    blocks = got[...].astype(F32)
     for zh in range(nzh):
         for zl in range(nzl):
             for c in range(CORES):
                 source = (zh * nzl + zl) * CORES + c
                 target = (zl * nzh + zh) * CORES + c
-                block = got[source * SUB : (source + 1) * SUB, :].astype(F32)
+                block = blocks[source * SUB : (source + 1) * SUB, :]
                 block = jnp.where(same, jnp.concatenate([block] * groups, axis=0), 0.0)
                 put = to_lane == target * slots + from_lane % slots
                 total = total + jnp.dot(

time: 117 us -> 117 us (level)
  no operation moved by 1% of the time
where the time goes in v6:
time: 117 us; the launch traced here: 116 us
  blocking collectives  49.9 us (43%)
  starting transfers between devices  27.2 us (23%)
  Pallas kernels  16.9 us (14%)
  waiting for transfers between devices  16.3 us (14%)
  local copies, waits for them, and re-layouts  5.07 us (4%)
    all_to_all x1, blocking collectives, per_device(): terms = lax.all_to_all(zh_message(terms, nzh), 'zh', 0, 0, tiled=True)  17 us
    all_to_all x1, starting transfers between devices, per_device(): first = lax.all_to_all(first, ('zh', 'zl', 'core'), 0, 0, tiled=True)  16.8 us
    all_to_all x1, blocking collectives, per_device(): beacons = lax.all_to_all(beacons, 'x', 0, 0, tiled=True)  11.4 us
    all_to_all x1, blocking collectives, per_device(): weights = lax.all_to_all(weights, ('dp', 'x'), 0, 0, tiled=True)  11.3 us
    pallas_call x8, Pallas kernels, small_call(): pl.pallas_call(kernel, in_specs=[SMEM if a.dtype == jnp.int32 else VMEM f...  10.7 us
    all_to_all x1, blocking collectives, per_device(): lax.all_to_all(spread(terms, nzl * CORES), ('zl', 'core'), 0, 0, tiled=True)  10.2 us
    all_to_all x1, waiting for transfers between devices, per_device(): first = lax.all_to_all(first, ('zh', 'zl', 'core'), 0, 0, tiled=True)  10.1 us
    all_to_all x1, waiting for transfers between devices, per_device(): lax.all_to_all(terms, ('x', 'zh', 'zl', 'core'), 0, 0, tiled=True, axis_i...  5.56 us
  transfers between devices with their start and end apart: 4, of which 3 were waited for; matrix products, arithmetic and copies ran while one was open for 0% of the time, Pallas kernels for 5%

profile of v6, /device:TPU:1, one launch (start us, length us, event | category | flops | bytes accessed | tf_op | source)
XLA Modules:
  0.0 116.2 jit_solution(3301891687840124927)
XLA Ops:
  0.6 1.8 %message.1 = bf16[256,384]{1,0:T(8,128)(2,1)} custom-call(bf16[8,256]{1,0:T(8,128)(2,1)} %bitcast.33, bf16[8,256]{1,0:T(8,128)(2,1)} %bitcast.34, bf16[8,3584]{1,0:T(8,128)(2,1)} %bitcast.32), custom_call_target="tpu_custom_call" | custom-call | bytes 524288 | tf_op jit(solution)/shard_map/message/pallas_call | solution.py:246
  2.4 16.8 %all-to-all-start = ((bf16[32,8,384]{2,1,0:T(8,128)(2,1)}), bf16[32,8,384]{2,1,0:T(8,128)(2,1)S(1)}, u32[]{:S(2)}, u32[]{:S(2)}) async-start(bf16[32,8,384]{2,1,0:T(8,128)(2,1)} %bitcast.31), calls=%async_computation | async-start | bytes 393216 | tf_op jit(solution)/shard_map/all_to_all | solution.py:448
  19.2 0.0 copy-start
  19.2 1.0 copy-done
  20.2 0.0 copy-start.1
  20.2 1.0 copy-done.1
  21.2 0.0 copy-start.2
  21.2 0.8 copy-done.2
  22.1 0.0 copy-start.3
  22.1 0.8 copy-done.3
  22.9 0.1 split_heads.1
  23.0 2.1 %collective-permute-start = (bf16[128,2048]{1,0:T(8,128)(2,1)S(1)}, bf16[128,2048]{1,0:T(8,128)(2,1)S(1)}, u32[]{:S(2)}, u32[]{:S(2)}) collective-permute-start(bf16[128,2048]{1,0:T(8,128)(2,1)S(1)} %get-tuple-element.29), channel_id=1, source_target_pairs={{0,1},{1,0},{2,3},{3,2},{4,5},{5,4},{6,7},{7,6},{8,9},{9,8},{10,11... | collective-permute-start | bytes 1572872 | tf_op jit(solution)/shard_map/ppermute | solution.py:450
  25.2 0.0 copy-start.4
  25.2 0.6 copy-done.4
  25.8 0.0 copy-start.5
  25.8 0.7 copy-done.5
  26.5 1.2 %mask.1.bias = f32[2,1024,128]{2,1,0:T(8,128)S(1)} custom-call(s32[128]{0:T(128)S(1)} %copy-done.4, s32[1,128]{1,0:T(1,128)S(1)} %bitcast.29, s32[1,128]{1,0:T(1,128)S(1)} %bitcast.30), custom_call_target="tpu_custom_call" | custom-call | bytes 2097152 | tf_op jit(solution)/shard_map/mask/pallas_call | solution.py:308
  27.7 0.0 collective-permute-done.other
  27.7 10.1 %all-to-all-done = bf16[32,8,384]{2,1,0:T(8,128)(2,1)S(1)} async-done(((bf16[32,8,384]{2,1,0:T(8,128)(2,1)}), bf16[32,8,384]{2,1,0:T(8,128)(2,1)S(1)}, u32[]{:S(2)}, u32[]{:S(2)}) %all-to-all-start) | async-done | bytes 196640 | tf_op jit(solution)/shard_map/all_to_all | solution.py:448
  37.9 11.4 %all_to_all.30 = bf16[4,256,256]{2,1,0:T(8,128)(2,1)S(1)} all-to-all(bf16[4,256,256]{2,1,0:T(8,128)(2,1)S(1)} %broadcast_in_dim.23), channel_id=1, replica_groups=mesh['dp'=4,'x'=4,'zh'=4,'zl'=4,'core'=2] {'x'}, dimensions={0} | all-to-all | bytes 1048576 | tf_op jit(solution)/shard_map/all_to_all | solution.py:456
  49.3 8.3 %attention.1 = (bf16[1024,256]{1,0:T(8,128)(2,1)}, bf16[1152,1792]{1,0:T(8,128)(2,1)}, bf16[128,1792]{1,0:T(8,128)(2,1)S(1)}) custom-call(f32[2,1024,128]{2,1,0:T(8,128)S(1)} %mask.1.bias, bf16[128,2048]{1,0:T(8,128)(2,1)S(1)} %get-tuple-element.31.mine, bf16[128,2048]{1,0:T(8,128)(2,1)S(1)} %collective-permute-done.other, bf16[1024,256]{1,0:T(8,128)(2,1)S(1)} %bitcast.22), custom_call_target="tpu_custom_call" | custom-call | flops 2113929216 | bytes 7733248 | tf_op jit(solution)/shard_map/attention/pallas_call | solution.py:192
  57.6 4.0 %all-to-all-start.2 = ((bf16[16,64,256]{2,1,0:T(8,128)(2,1)}), bf16[16,64,256]{2,1,0:T(8,128)(2,1)S(1)}, u32[]{:S(2)}, u32[]{:S(2)}) async-start(bf16[16,64,256]{2,1,0:T(8,128)(2,1)} %bitcast.12), calls=%async_computation.2 | async-start | bytes 1048576 | tf_op jit(solution)/shard_map/all_to_all | solution.py:462
  61.5 3.2 %own_grads.1 = (bf16[128,1152]{1,0:T(8,128)(2,1)S(1)}, bf16[128,1152]{1,0:T(8,128)(2,1)S(1)}) custom-call(bf16[1152,1792]{1,0:T(8,128)(2,1)} %get-tuple-element.35.dscores, bf16[128,1792]{1,0:T(8,128)(2,1)S(1)} %get-tuple-element.36.probs, bf16[128,2048]{1,0:T(8,128)(2,1)S(1)} %get-tuple-element.31.mine, bf16[128,2048]{1,0:T(8,128)(2,1)S(1)} %collective-permute-done.other, ...), custom_call_target="tpu_custom_call" | custom-call | flops 528482304 | bytes 6291456 | tf_op jit(solution)/shard_map/own_grads/pallas_call | solution.py:133
  64.8 4.4 %collective-permute-start.1 = (bf16[128,1152]{1,0:T(8,128)(2,1)S(1)}, bf16[128,1152]{1,0:T(8,128)(2,1)S(1)}, u32[]{:S(2)}, u32[]{:S(2)}) collective-permute-start(bf16[128,1152]{1,0:T(8,128)(2,1)S(1)} %get-tuple-element.38), channel_id=1, source_target_pairs={{0,1},{1,0},{2,3},{3,2},{4,5},{5,4},{6,7},{7,6},{8,9},{9,8},{10,11... | collective-permute-start | bytes 884744 | tf_op jit(solution)/shard_map/ppermute | solution.py:467
  69.2 0.6 turn.1.hidden
  69.7 0.6 collective-permute-done.1.got
  70.3 0.9 join_heads.1
  71.2 5.6 %all-to-all-done.2.got = bf16[16,64,256]{2,1,0:T(8,128)(2,1)S(1)} async-done(((bf16[16,64,256]{2,1,0:T(8,128)(2,1)}), bf16[16,64,256]{2,1,0:T(8,128)(2,1)S(1)}, u32[]{:S(2)}, u32[]{:S(2)}) %all-to-all-start.2) | async-done | bytes 524320 | tf_op jit(solution)/shard_map/all_to_all | solution.py:462
  76.8 0.1 zh_message.1
  76.8 17.0 %all_to_all.31.got = bf16[4,80,128]{2,1,0:T(8,128)(2,1)S(1)} all-to-all(bf16[4,80,128]{2,1,0:T(8,128)(2,1)S(1)} %zh_message.1), channel_id=1, replica_groups=mesh['dp'=4,'x'=4,'zh'=4,'zl'=4,'core'=2] {'zh'}, dimensions={0} | all-to-all | bytes 163840 | tf_op jit(solution)/shard_map/all_to_all | solution.py:472
  93.9 10.2 %all_to_all.32.got = bf16[8,80,128]{2,1,0:T(8,128)(2,1)S(1)} all-to-all(bf16[8,80,128]{2,1,0:T(8,128)(2,1)S(1)} %spread.1), channel_id=1, replica_groups=mesh['dp'=4,'x'=4,'zh'=4,'zl'=4,'core'=2] {'zl','core'}, dimensions={0} | all-to-all | bytes 327680 | tf_op jit(solution)/shard_map/all_to_all | solution.py:473
  104.1 0.2 weight_terms.1
  104.3 11.3 %all_to_all.33.weights = bf16[16,8,256]{2,1,0:T(8,128)(2,1)S(1)} all-to-all(bf16[16,8,256]{2,1,0:T(8,128)(2,1)S(1)} %bitcast.26), channel_id=1, replica_groups=mesh['dp'=4,'x'=4,'zh'=4,'zl'=4,'core'=2] {'dp','x'}, dimensions={0} | all-to-all | bytes 131072 | tf_op jit(solution)/shard_map/all_to_all | solution.py:476
  115.6 0.6 finish.1
  (4 shorter events, 0.1 us)
Async XLA Ops:
  2.4 35.4 %all-to-all-start = ((bf16[32,8,384]{2,1,0:T(8,128)(2,1)}), bf16[32,8,384]{2,1,0:T(8,128)(2,1)S(1)}, u32[]{:S(2)}, u32[]{:S(2)}) async-start(bf16[32,8,384]{2,1,0:T(8,128)(2,1)} %bitcast.31), calls=%async_computation | async-start | bytes 393216 | tf_op jit(solution)/shard_map/all_to_all | solution.py:448
  19.2 1.0 copy-start
  20.2 1.0 copy-start.1
  21.2 0.8 copy-start.2
  22.1 0.8 copy-start.3
  23.0 4.7 %collective-permute-start = (bf16[128,2048]{1,0:T(8,128)(2,1)S(1)}, bf16[128,2048]{1,0:T(8,128)(2,1)S(1)}, u32[]{:S(2)}, u32[]{:S(2)}) collective-permute-start(bf16[128,2048]{1,0:T(8,128)(2,1)S(1)} %get-tuple-element.29), channel_id=1, source_target_pairs={{0,1},{1,0},{2,3},{3,2},{4,5},{5,4},{6,7},{7,6},{8,9},{9,8},{10,11... | collective-permute-start | bytes 1572872 | tf_op jit(solution)/shard_map/ppermute | solution.py:450
  25.2 0.7 copy-start.4
  25.8 0.7 copy-start.5
  57.6 19.2 %all-to-all-start.2 = ((bf16[16,64,256]{2,1,0:T(8,128)(2,1)}), bf16[16,64,256]{2,1,0:T(8,128)(2,1)S(1)}, u32[]{:S(2)}, u32[]{:S(2)}) async-start(bf16[16,64,256]{2,1,0:T(8,128)(2,1)} %bitcast.12), calls=%async_computation.2 | async-start | bytes 1048576 | tf_op jit(solution)/shard_map/all_to_all | solution.py:462
  64.8 5.5 %collective-permute-start.1 = (bf16[128,1152]{1,0:T(8,128)(2,1)S(1)}, bf16[128,1152]{1,0:T(8,128)(2,1)S(1)}, u32[]{:S(2)}, u32[]{:S(2)}) collective-permute-start(bf16[128,1152]{1,0:T(8,128)(2,1)S(1)} %get-tuple-element.38), channel_id=1, source_target_pairs={{0,1},{1,0},{2,3},{3,2},{4,5},{5,4},{6,7},{7,6},{8,9},{9,8},{10,11... | collective-permute-start | bytes 884744 | tf_op jit(solution)/shard_map/ppermute | solution.py:467
